TPU v7x, 512 devices: a whole 4x4x16 slice. The times are simulated.
512 devices in a mesh: slot: 64 (over y, z), tp: 8 (over x, core).
Axes of the slice: x: 4, y: 4, z: 16, core: 2. Of those that a mesh axis runs over, the one named last changes fastest.
Arguments:
- x_in: bfloat16 [49152, 8192], P('slot', 'tp'), may hold values from -6 to 6
- bc_in: bfloat16 [49152, 2048], P('slot', 'tp'), may hold values from -6 to 6
- z_gate: bfloat16 [49152, 8192], P('slot', 'tp'), may hold values from -60 to 60
- decay_rate: float32 [49152, 128], P('slot', 'tp'), may hold values from 0 to 2, as said below
- step_size: float32 [49152, 128], P('slot', 'tp'), may hold values from 0 to 1, as said below
- d_skip: float32 [128], P('tp'), may hold values from 0.5 to 1.5
- conv_x: float32 [4, 8192], P(None, 'tp'), may hold values from -3 to 3
- conv_bc: float32 [4, 2048], P(None, 'tp'), may hold values from -3 to 3
- norm_weight: float32 [8192], P('tp'), may hold values from 0.5 to 1.5
- lengths: int32 [4], replicated, may hold values from 1 to 24576, as said below
Outputs:
- gated_out: bfloat16 [49152, 8192], P('slot', 'tp')
Inputs may be any that keep to these rules, and one draw needn't show every extreme that they name: prompt lengths in token order, laid end to end from token 0; the first prompt has 1536 to 12288 tokens and the second exactly 24576. `decay_rate`: positive. `step_size`: positive.
All inputs are finite; a program needn't handle non-finite values.
Results may differ from a plain program's by a relative error of at most 0.0055.
Values may be sent and summed in bfloat16 or wider, within the bound.
A program may use at most 128 MiB of HBM per device.

v0:
```python
import jax
import jax.numpy as jnp
from jax import lax
from jax.sharding import PartitionSpec as P

SPACE_HEADS = 128
HEAD_DIM = 64
STATE = 128
CONV = 4


EPSILON = 1e-05


def from_behind(block, axis, distance):
    devices = range(lax.axis_size(axis))
    route = [(i - distance, i) for i in devices if i - distance in devices]
    return lax.ppermute(block, axis, route)


def carried_in(array, axis, combine, identity):
    size, here = (lax.axis_size(axis), lax.axis_index(axis))
    everything = jax.tree.map(lambda part: lax.all_gather(part, axis), array)
    start = jax.tree.map(
        lambda part, zero: jnp.broadcast_to(jnp.asarray(zero, part.dtype), part.shape),
        array,
        identity,
    )

    def step(k, before):
        reached = k < here
        new = combine(before, jax.tree.map(lambda part: part[k], everything))
        return jax.tree.map(lambda a, b: jnp.where(reached, a, b), new, before)

    return lax.fori_loop(0, size, step, start)


def segment_of(positions, prompt_ends):
    return jnp.sum(
        (positions[:, None] >= prompt_ends[None, :]).astype(jnp.int32), axis=1, dtype=jnp.int32
    )


def conv_block(rim_rows, values_in, rim_seg, segment, weight):
    block_rows = values_in.shape[0]
    extended = jnp.concatenate([rim_rows, values_in], axis=0).astype(jnp.float32)
    ext_seg = jnp.concatenate([rim_seg, segment], axis=0)
    summed = weight[CONV - 1] * extended[CONV - 1 :]
    for tap_index in range(CONV - 1):
        shifted = extended[tap_index : tap_index + block_rows]
        same_prompt = (ext_seg[tap_index : tap_index + block_rows] == segment)[:, None]
        summed = summed + weight[tap_index] * jnp.where(same_prompt, shifted, 0.0)
    return jax.nn.silu(summed).astype(jnp.bfloat16)


def span_terms(x_conv, bc_conv, rate_blk, step_blk, seg_blk, first_blk, d_skip):
    block_rows = x_conv.shape[0]
    head_count = rate_blk.shape[1]
    group_count = bc_conv.shape[1] // (2 * STATE)
    per_group = head_count // group_count
    head_vals = x_conv.reshape(block_rows, head_count, HEAD_DIM)
    paired = bc_conv.reshape(block_rows, group_count, 2, STATE)
    key_rows = paired[:, :, 0]
    queries = paired[:, :, 1]
    cum_rate = jnp.cumsum(rate_blk, axis=0)
    scores = jnp.einsum("tgn,sgn->gts", queries, key_rows, preferred_element_type=jnp.float32)
    order_idx = jnp.arange(block_rows, dtype=jnp.int32)
    visible = (order_idx[:, None] >= order_idx[None, :]) & (seg_blk[:, None] == seg_blk[None, :])

    def pair_fn(pair_index):
        first_head = pair_index * 2
        group_index = first_head // per_group
        group_scores = lax.dynamic_index_in_dim(scores, group_index, 0, keepdims=False)
        cum_pair = lax.dynamic_slice_in_dim(cum_rate, first_head, 2, 1).T
        step_pair = lax.dynamic_slice_in_dim(step_blk, first_head, 2, 1).T
        differ = cum_pair[:, :, None] - cum_pair[:, None, :]
        decays = jnp.where(visible[None], jnp.exp(-jnp.where(visible[None], differ, 0.0)), 0.0)
        weights = (group_scores[None] * decays * step_pair[:, None, :]).astype(jnp.bfloat16)
        pair_vals = lax.dynamic_slice_in_dim(head_vals, first_head, 2, 1)
        return jnp.einsum("hts,shp->thp", weights, pair_vals, preferred_element_type=jnp.float32)

    y_pairs = lax.map(pair_fn, jnp.arange(head_count // 2, dtype=jnp.int32))
    y_local = y_pairs.transpose(1, 0, 2, 3).reshape(block_rows, head_count, HEAD_DIM)
    y_local = y_local + d_skip[None, :, None] * head_vals.astype(jnp.float32)
    last_prompt = seg_blk[block_rows - 1]
    to_end = (
        jnp.where(
            (seg_blk == last_prompt)[:, None],
            jnp.exp(-(cum_rate[block_rows - 1][None, :] - cum_rate)),
            0.0,
        )
        * step_blk
    )
    scaled = (to_end[:, :, None] * head_vals.astype(jnp.float32)).astype(jnp.bfloat16)
    state_local = jnp.einsum(
        "sgrp,sgn->grpn",
        scaled.reshape(block_rows, group_count, per_group, HEAD_DIM),
        key_rows,
        preferred_element_type=jnp.float32,
    )
    state_local = state_local.reshape(head_count, HEAD_DIM, STATE)
    before_start = jnp.cumsum(first_blk.astype(jnp.int32), dtype=jnp.int32) == 0
    carry_in = jnp.where(before_start[:, None], jnp.exp(-cum_rate), 0.0)
    block_decay = jnp.where(jnp.any(first_blk), 0.0, jnp.exp(-cum_rate[block_rows - 1]))
    return (y_local, state_local, block_decay, carry_in, queries)


def add_carried(y_local, queries, carry_in, carried):
    block_rows, head_count = carry_in.shape
    group_count = queries.shape[1]
    carried_b = carried.astype(jnp.bfloat16).reshape(
        group_count, head_count // group_count, HEAD_DIM, STATE
    )
    carried_out = jnp.einsum(
        "tgn,grpn->tgrp", queries, carried_b, preferred_element_type=jnp.float32
    )
    return y_local + carry_in[:, :, None] * carried_out.reshape(block_rows, head_count, HEAD_DIM)


def link_states(earlier, later):
    return (earlier[0] * later[0], later[0][:, None, None] * earlier[1] + later[1])


def body(x_in, bc_in, z_gate, decay_rate, step_size, d_skip, conv_x, conv_bc, norm_weight, lengths):
    row_count = x_in.shape[0]
    rim_width = CONV - 1
    first_row = lax.axis_index("slot") * row_count
    positions = first_row + jnp.arange(row_count, dtype=jnp.int32)
    prompt_ends = jnp.cumsum(lengths, dtype=jnp.int32)
    prompt_starts = prompt_ends - lengths
    segment = segment_of(positions, prompt_ends)
    first_token = jnp.any(positions[:, None] == prompt_starts[None, :], axis=1)
    rim_x, rim_bc = from_behind(
        (x_in[row_count - rim_width :], bc_in[row_count - rim_width :]), "slot", 1
    )
    rim_seg = segment_of(
        first_row - rim_width + jnp.arange(rim_width, dtype=jnp.int32), prompt_ends
    )
    x_conv = conv_block(rim_x, x_in, rim_seg, segment, conv_x)
    bc_conv = conv_block(rim_bc, bc_in, rim_seg, segment, conv_bc)
    head_count = decay_rate.shape[1]
    block_list = span_terms(x_conv, bc_conv, decay_rate, step_size, segment, first_token, d_skip)
    device_decay = jnp.ones((head_count,), jnp.float32)
    device_state = jnp.zeros((head_count, HEAD_DIM, STATE), jnp.float32)
    device_state = block_list[2][:, None, None] * device_state + block_list[1]
    device_decay = device_decay * block_list[2]
    identity = (
        jnp.ones((head_count,), jnp.float32),
        jnp.zeros((head_count, HEAD_DIM, STATE), jnp.float32),
    )
    incoming = carried_in((device_decay, device_state), "slot", link_states, identity)[1]
    outputs = add_carried(block_list[0], block_list[4], block_list[3], incoming)
    y_all = outputs.reshape(row_count, -1)
    gated_rows = y_all * jax.nn.silu(z_gate.astype(jnp.float32))
    total_sq = lax.psum(jnp.sum(gated_rows * gated_rows, axis=1), "tp")
    mean_sq = total_sq / (SPACE_HEADS * HEAD_DIM)
    return (gated_rows * lax.rsqrt(mean_sq + EPSILON)[:, None] * norm_weight).astype(jnp.bfloat16)


def solution(mesh):
    placed = (
        P("slot", "tp"),
        P("slot", "tp"),
        P("slot", "tp"),
        P("slot", "tp"),
        P("slot", "tp"),
        P("tp"),
        P(None, "tp"),
        P(None, "tp"),
        P("tp"),
        P(),
    )
    return jax.shard_map(
        body, mesh=mesh, in_specs=placed, out_specs=P("slot", "tp"), check_vma=False
    )
```

profile of v0, /device:TPU:1, one launch (start us, length us, event | category | flops | bytes accessed | tf_op | source)
XLA Modules:
  0.0 440.0 jit_solution(5445253929646253009)
XLA Ops:
  7.5 4.4 collective-permute-start
  12.8 3.5 collective-permute-start.1
  16.3 1.7 reduce-window.30
  27.0 1.7 copy.39
  30.8 3.5 fusion.14
  34.3 1.4 convolution_add_fusion
  35.8 2.6 copy.46
  38.5 70.1 %all-gather.1 = f32[64,1,16]{2,1,0:T(1,128)S(1)} all-gather(f32[1,1,16]{2,1,0:T(1,128)S(1)} %bitcast.134), channel_id=1, replica_groups=mesh['slot'=64,'tp'=8] {'slot'}, dimensions={0}, use_global_device_ids=true | all-gather | bytes 4160 | tf_op jit(solution)/shard_map/all_gather | solution.py:23
  108.6 1.9 convolution_bitcast_fusion
  110.5 52.3 %while.25 = (s32[]{:T(128)}, f32[8,768,2,64]{1,3,2,0:T(8,128)}, s32[8]{0:T(128)S(1)}, bf16[768,16,64]{0,2,1:T(8,128)(2,1)S(1)}, f32[1,768,768]{2,1,0:T(8,128)}, ...) while((s32[]{:T(128)}, f32[8,768,2,64]{1,3,2,0:T(8,128)}, ...), condition=%wide.region_6.7_spmd.clone, body=%wide.region_5.6_spmd.clone.sunk | while | flops 161021952 | bytes 4175043 | solution.py:82
  112.9 4.1 fusion.53
  119.4 4.1 fusion.53
  125.9 4.1 fusion.53
  132.4 4.4 %fusion.53 = f32[8,768,2,64]{1,3,2,0:T(8,128)} fusion(f32[8,768,2,64]{1,3,2,0:T(8,128)} %get-tuple-element.356, s32[]{:T(128)S(6)} %copy.67, f32[2,768]{1,0:T(2,128)S(1)} %get-tuple-element.315, f32[2,768]{1,0:T(2,128)S(1)} %get-tuple-element.316, f32[768,768]{1,0:T(8,128)} %bitcast.121, pred[768,768]{1,0:T(8,128)(4,1)S(1)} %fusion.52, ...), kind=kOutput, calls=%fused_computation.7.clone.1 | convolution fusion | flops 159252480 | bytes 3557384 | tf_op jit(solution)/shard_map/while/body/eval_jaxpr/hts,shp->thp/dot_general | solution.py:80
  139.2 4.1 fusion.53
  145.7 4.1 fusion.53
  152.2 4.1 fusion.53
  158.7 4.1 fusion.53
  162.8 170.0 %all-gather.4.cloned.1.call-done = f32[1024,64,128]{2,1,0:T(8,128)} async-done(((f32[16,64,128]{2,1,0:T(8,128)}), f32[1024,64,128]{2,1,0:T(8,128)}) %all-gather.4.cloned.1.call-update) | async-done | bytes 33554448 | tf_op jit(solution)/shard_map/all_gather | solution.py:23
  332.8 77.9 %while.26 = (s32[]{:T(128)}, f32[16,64,128]{2,1,0:T(8,128)S(1)}, s32[]{:T(128)}, f32[64,16]{1,0:T(8,128)S(1)}, f32[64,16,64,128]{3,2,1,0:T(8,128)}, /*index=5*/s32[]{:T(128)}, s32[]{:T(128)}) while((s32[]{:T(128)}, f32[16,64,128]{2,1,0:T(8,128)S(1)}, s32[]{:T(128)}, f32[64,16]{1,0:T(8,128)S(1)}, f32[64,16,64,128]{3,2,1,0:T(8,128)}, ...), condition=%wide.region_12.13_spmd.clone, body=%wide.region_11.12_spmd.clone.sunk | while | flops 524292 | bytes 1573169 | solution.py:35
  335.3 1.2 fusion.54
  337.7 1.2 fusion.54
  338.9 1.2 fusion.54
  341.4 1.2 fusion.54
  343.8 1.2 fusion.54
  345.0 1.2 fusion.54
  347.5 1.2 fusion.54
  349.9 1.2 fusion.54
  352.3 1.2 fusion.54
  353.5 1.2 fusion.54
  356.0 1.2 fusion.54
  358.4 1.2 fusion.54
  360.9 1.2 fusion.54
  362.1 1.2 fusion.54
  364.5 1.2 fusion.54
  366.9 1.2 fusion.54
  368.2 1.2 fusion.54
  370.6 1.2 fusion.54
  373.0 1.2 fusion.54
  375.5 1.2 fusion.54
  376.7 1.2 fusion.54
  379.1 1.2 fusion.54
  381.5 1.2 fusion.54
  384.0 1.2 fusion.54
  412.6 3.6 multiply_reduce_fusion
  416.2 12.9 %psum.7 = f32[768]{0:T(1024)S(1)} all-reduce(f32[768]{0:T(1024)S(1)} %get-tuple-element.218), channel_id=1, replica_groups=mesh['slot'=64,'tp'=8] {'tp'}, use_global_device_ids=true, to_apply=%region_14.15 | all-reduce | flops 768 | bytes 6144 | tf_op jit(solution)/shard_map/psum | solution.py:155
  429.1 1.5 multiply_convert_fusion.6
  430.6 2.6 copy.47
  (186 shorter events, 76.2 us)
Async XLA Ops:
  6.5 9.8 %copy-start = (f32[768,16]{0,1:T(8,128)S(1)}, f32[768,16]{0,1:T(8,128)}, u32[]{:S(2)}) copy-start(f32[768,16]{0,1:T(8,128)} %param.17) | copy-start | bytes 147460
  6.5 22.2 %copy-start.4 = (bf16[768,256]{1,0:T(8,128)(2,1)S(1)}, bf16[768,256]{1,0:T(8,128)(2,1)}, u32[]{:S(2)}) copy-start(bf16[768,256]{1,0:T(8,128)(2,1)} %param.15) | copy-start | bytes 1179652
  6.5 326.3 %all-gather.4.cloned.1.call-start = ((), (), s32[]{:S(2)}) async-start(), calls=%async_computation | async-start | bytes 34078720 | tf_op jit(solution)/shard_map/all_gather | solution.py:23
  7.5 22.5 %collective-permute-start = (bf16[3,1024]{0,1:T(8,128)(2,1)S(1)}, bf16[3,1024]{0,1:T(8,128)(2,1)S(1)}, u32[]{:S(2)}, u32[]{:S(2)}) collective-permute-start(bf16[3,1024]{0,1:T(8,128)(2,1)S(1)} %copy.38), channel_id=1, source_target_pairs={{0,8},{8,16},{16,24},{24,32},{32,40},{40,48},{48,56},{56,64},{64,7... | collective-permute-start | bytes 18440 | tf_op jit(solution)/shard_map/ppermute | solution.py:18
  12.8 16.2 %collective-permute-start.1 = (bf16[3,256]{0,1:T(8,128)(2,1)S(1)}, bf16[3,256]{0,1:T(8,128)(2,1)S(1)}, u32[]{:S(2)}, u32[]{:S(2)}) collective-permute-start(bf16[3,256]{0,1:T(8,128)(2,1)S(1)} %copy.40), channel_id=1, source_target_pairs={{0,8},{8,16},{16,24},{24,32},{32,40},{40,48},{48,56},{56,64},{64,7... | collective-permute-start | bytes 4616 | tf_op jit(solution)/shard_map/ppermute | solution.py:18
  34.3 4.0 copy-start.6
  162.8 170.0 %copy-start.1 = (bf16[768,16,64]{0,2,1:T(8,128)(2,1)}, bf16[768,16,64]{0,2,1:T(8,128)(2,1)S(1)}, u32[]{:S(2)}) copy-start(bf16[768,16,64]{0,2,1:T(8,128)(2,1)S(1)} %get-tuple-element.380) | copy-start | bytes 4718596
  410.7 1.4 copy-start.2
  410.7 1.9 copy-start.3
  412.6 16.5 %copy-start.5 = (f32[1024]{0:T(1024)S(1)}, f32[1024]{0:T(1024)}, u32[]{:S(2)}) copy-start(f32[1024]{0:T(1024)} %param.22) | copy-start | bytes 12292
Sparse Core Ops, SparseCore 0:
  35.9 296.9 all-gather.3
where the time goes:
time: 444 us; the launch traced here: 440 us
  waiting for transfers between devices  170 us (38%)
  other arithmetic  96.4 us (22%)
  blocking collectives  83 us (19%)
  matrix products  37.1 us (8%)
  local copies, waits for them, and re-layouts  24.6 us (6%)
  between operations  13.6 us (3%)
  starting transfers between devices  7.92 us (2%)
  loops' own time  7.46 us (2%)
    all_gather x1, waiting for transfers between devices, carried_in(): everything = jax.tree.map(lambda part: lax.all_gather(part, axis), array)  170 us
    select_n x64, other arithmetic, step(): return jax.tree.map(lambda a, b: jnp.where(reached, a, b), new, before)  75 us
    all_gather x1, blocking collectives, carried_in(): everything = jax.tree.map(lambda part: lax.all_gather(part, axis), array)  70.1 us
    dot_general x8, matrix products, pair_fn(): jnp.einsum('hts,shp->thp', weights, pair_vals, preferred_element_type=jnp...  33.2 us
    psum x1, blocking collectives, body(): total_sq = lax.psum(jnp.sum(gated_rows * gated_rows, axis=1), 'tp')  12.9 us
  transfers between devices with their start and end apart: 3, of which 1 were waited for; matrix products, arithmetic and copies ran while one was open for 15% of the time, Pallas kernels for 0%

commit v1 on v0

v1 whole, which is shorter than its diff:
```python
import functools

import jax
import jax.numpy as jnp
from jax import lax
from jax.experimental import pallas as pl
from jax.experimental.pallas import tpu as pltpu
from jax.sharding import PartitionSpec as P

MESH = pl.DeviceIdType.MESH
HEAD_DIM = 64
STATE = 128
SUB = 64
PARTS = 4
WIDE = 256
QUADS = 16
EPSILON = 1e-05
F32 = jnp.float32
BF16 = jnp.bfloat16


def silu(v):
    half = 0.5 * v
    return half * jnp.tanh(half) + half


def dot(a, b):
    return jnp.dot(a, b, preferred_element_type=F32)


def exact_dot(a, b, dims):
    return lax.dot_general(
        a, b, (dims, ((), ())), precision=lax.Precision.HIGHEST, preferred_element_type=F32
    )


def iota(shape, axis):
    return lax.broadcasted_iota(jnp.int32, shape, axis)


def two_terms(v):
    high = v.astype(BF16).astype(F32)
    return jnp.where(iota(v.shape, 1) < 16, high, v - high).astype(BF16)


def kernel(
    tp_size,
    len_ref,
    x_hbm,
    bc_ref,
    z_hbm,
    rate_ref,
    step_ref,
    skip_ref,
    conv_x_ref,
    conv_bc_ref,
    norm_ref,
    out_hbm,
    xs,
    zs,
    bcs,
    shift_ref,
    left_ref,
    right_ref,
    keys_ref,
    c_ref,
    xconv,
    cum_ref,
    mid_ref,
    end_ref,
    f_ref,
    e_ref,
    ef_ref,
    rows_ref,
    y_ref,
    g_ref,
    sq_ref,
    o_ref,
    decay_all,
    decay_rows,
    decay_wide,
    l_send,
    q_recv,
    t_send,
    o_recv,
    o_send,
    g_recv,
    p_send,
    c_recv,
    n_send,
    n_recv,
    n_rows,
    in_sem,
    out_sem,
    halo_send,
    halo_recv,
    d_send1,
    d_recv1,
    d_send2,
    d_recv2,
    s1,
    r1,
    s2,
    r2,
    s3,
    r3,
    s4,
    r4,
    ns,
    nr,
):
    tokens = x_hbm.shape[0]
    subs = tokens // SUB
    slots = 4 * QUADS
    slot = lax.axis_index("slot")
    tp = lax.axis_index("tp")
    quad = slot // 4
    member = slot % 4
    first_row = slot * tokens
    after, before = (slot + 1) % slots, (slot + slots - 1) % slots

    def quad_peer(i):
        return quad * 4 + (member + i) % 4

    def far_peer(i):
        return ((quad + i) % QUADS) * 4 + member

    def x_copy(p):
        return pltpu.make_async_copy(
            x_hbm.at[:, pl.ds(p * WIDE, WIDE)], xs.at[p, pl.ds(16, tokens)], in_sem.at[p]
        )

    def z_copy(p):
        return pltpu.make_async_copy(
            z_hbm.at[:, pl.ds(p * WIDE, WIDE)], zs.at[p], in_sem.at[PARTS + p]
        )

    barrier = pltpu.get_barrier_semaphore()

    def greet(peer):
        pl.semaphore_signal(barrier, inc=1, device_id={"slot": peer}, device_id_type=MESH)

    greet(after)
    greet(before)
    for i in range(1, 4):
        greet(quad_peer(i))
    lax.fori_loop(1, QUADS, lambda i, c: (greet(far_peer(i)), c)[1], 0)
    for i in range(1, tp_size):
        pl.semaphore_signal(
            barrier, inc=1, device_id={"tp": (tp + i) % tp_size}, device_id_type=MESH
        )
    for p in range(PARTS):
        x_copy(p).start()
    for p in range(PARTS):
        z_copy(p).start()

    ends = []
    total = 0
    for i in range(4):
        total = total + len_ref[i]
        ends.append(total)

    def start_of(pos, bounds):
        start = jnp.zeros_like(pos)
        for end in bounds:
            start = jnp.where(pos >= end, end, start)
        return start

    twice = (iota((16, 32), 0) == iota((16, 32), 1) % 16).astype(F32)
    zero_one = iota((128, 128), 0), iota((128, 128), 1)
    tri = ((zero_one[0] >= zero_one[1]) & (zero_one[0] // SUB == zero_one[1] // SUB)).astype(F32)
    width = min(128, tokens)
    for b in range(tokens // width):
        rate = rate_ref[b * width : (b + 1) * width, :]
        rate = jnp.concatenate([rate, rate], axis=1)
        cum_ref[b * width : (b + 1) * width, :] = exact_dot(
            tri[:width, :width], rate, ((1,), (0,))
        )
    mid_ref[...] = jnp.zeros_like(mid_ref)
    end_ref[...] = jnp.zeros_like(end_ref)
    offset = jnp.zeros((1, 32), F32)
    for c in range(subs):
        at = slice(c * SUB, (c + 1) * SUB)
        cum = cum_ref[at, :]
        mid = cum_ref[c * SUB + 31 : c * SUB + 32, :]
        end = cum_ref[c * SUB + 63 : c * SUB + 64, :]
        mid_ref[c : c + 1, :] = mid
        end_ref[c : c + 1, :] = end
        step = step_ref[at, :]
        step = jnp.concatenate([step, step], axis=1)
        f_ref[at, :] = two_terms(jnp.exp(cum - mid) * step)
        e_ref[at, :] = two_terms(jnp.exp(mid - cum))
        pos = first_row + c * SUB + iota((SUB, 32), 0)
        open_rows = start_of(pos, ends[:3]) < first_row
        ef_ref[at, :] = two_terms(jnp.where(open_rows, jnp.exp(-(offset + cum)), 0.0))
        offset = offset + end
    last_pos = first_row + tokens - 1 + jnp.zeros((1, 32), jnp.int32)
    whole = start_of(last_pos, ends[:3]) < first_row
    decay = jnp.where(whole, jnp.exp(-offset), 0.0)
    decay_all[slot] = jnp.zeros((1, 128), F32)
    decay_all[slot, :, 0:32] = jnp.where(iota((1, 32), 1) < 16, decay, 0.0)
    g1 = jnp.exp(-mid_ref[...])
    g2 = jnp.exp(mid_ref[...] - end_ref[...])
    sub_pos = first_row + iota((16, 32), 0) * SUB
    keep = start_of(sub_pos + (SUB - 1), ends) < sub_pos
    rows_ref[0:16, :] = two_terms(g1)
    rows_ref[16:32, :] = two_terms(g2)
    rows_ref[32:48, :] = two_terms(jnp.where(keep, g2, 0.0))
    skip = skip_ref[...]
    rows_ref[48:64, :] = two_terms(
        jnp.broadcast_to(jnp.concatenate([skip, skip], axis=1), (16, 32))
    )

    for c in range(subs):
        base = first_row + c * SUB
        t = iota((SUB, 80), 0)
        s = iota((SUB, 80), 1) - 16
        inside = (base + s) >= start_of(base + t, ends)
        for d in range(1, 4):
            shift_ref[c, (d - 1) * SUB : d * SUB, :] = ((s == t - d) & inside).astype(F32).astype(BF16)

    pl.semaphore_wait(barrier, 2 + 3 + (QUADS - 1) + (tp_size - 1))
    halos = []
    for p in range(PARTS):
        halos.append(
            pltpu.make_async_remote_copy(
                x_hbm.at[pl.ds(tokens - 16, 16), pl.ds(p * WIDE, WIDE)],
                xs.at[p, pl.ds(0, 16)],
                halo_send.at[p],
                halo_recv.at[p],
                device_id={"slot": after},
                device_id_type=MESH,
            )
        )
    halos.append(
        pltpu.make_async_remote_copy(
            bc_ref.at[pl.ds(tokens - 16, 16)],
            bcs.at[pl.ds(0, 16)],
            halo_send.at[PARTS],
            halo_recv.at[PARTS],
            device_id={"slot": after},
            device_id_type=MESH,
        )
    )
    halos[PARTS].start()
    for p in range(PARTS):
        halos[p].start()

    def near_decay(i):
        return pltpu.make_async_remote_copy(
            decay_all.at[slot],
            decay_all.at[slot],
            d_send1.at[i],
            d_recv1.at[i],
            device_id={"slot": quad_peer(i)},
            device_id_type=MESH,
        )

    def far_decay(i):
        return pltpu.make_async_remote_copy(
            decay_all.at[pl.ds(quad * 4, 4)],
            decay_all.at[pl.ds(quad * 4, 4)],
            d_send2.at[i],
            d_recv2.at[i],
            device_id={"slot": far_peer(i)},
            device_id_type=MESH,
        )

    for i in range(1, 4):
        near_decay(i).start()

    bcs[16:, :] = bc_ref[...]
    halos[PARTS].wait_recv()

    def conv(rows, shifts, taps):
        moved = dot(shifts, rows)
        summed = taps[3:4] * rows[16:].astype(F32)
        for d in range(1, 4):
            summed = summed + taps[3 - d : 4 - d] * moved[(d - 1) * SUB : d * SUB]
        return silu(summed).astype(BF16)

    for c in range(subs):
        base = first_row + c * SUB
        bc = conv(bcs[c * SUB : c * SUB + 80, :], shift_ref[c], conv_bc_ref[...])
        key, query = bc[:, :STATE], bc[:, STATE:]
        c_ref[c * SUB : (c + 1) * SUB, :] = query
        scores = lax.dot_general(query, key, (((1,), (1,)), ((), ())), preferred_element_type=F32)
        t = iota((SUB, SUB), 0)
        s = iota((SUB, SUB), 1)
        seen = (t >= s) & ((base + s) >= start_of(base + t, ends))
        left_ref[c, :, STATE:] = jnp.where(seen, scores, 0.0).astype(BF16)
        row = base + iota((SUB, STATE), 0)
        from_before = start_of(row, ends) < base
        left_ref[c, :, :STATE] = jnp.where(from_before, query.astype(F32), 0.0).astype(BF16)
        last = start_of(jnp.zeros((SUB, STATE), jnp.int32) + (base + SUB - 1), ends)
        keys = jnp.where(row >= last, key.astype(F32), 0.0)
        keys_ref[c] = keys.T.astype(BF16)

    for i in range(1, 4):
        near_decay(i).wait_recv()
    lax.fori_loop(1, QUADS, lambda i, c: (far_decay(i).start(), c)[1], 0)

    def widen_matrix(p, rows):
        r = iota((rows, WIDE), 0) % 16
        return (r == 4 * p + iota((rows, WIDE), 1) // HEAD_DIM).astype(F32).astype(BF16)

    def states(p):
        x_copy(p).wait()
        pltpu.make_async_remote_copy(
            x_hbm.at[pl.ds(tokens - 16, 16), pl.ds(0, WIDE)],
            xs.at[p, pl.ds(0, 16)],
            halo_send.at[p],
            halo_recv.at[p],
            device_id={"slot": after},
            device_id_type=MESH,
        ).wait_recv()
        taps = conv_x_ref[p]
        matrix = widen_matrix(p, 32)
        rows = dot(rows_ref[...], matrix)
        state = jnp.zeros((STATE, WIDE), F32)
        for c in range(subs):
            at = slice(c * SUB, (c + 1) * SUB)
            values = conv(xs[p, c * SUB : c * SUB + 80, :], shift_ref[c], taps)
            xconv[p, at, :] = values
            scaled = (values.astype(F32) * dot(f_ref[at, :], matrix)).astype(BF16)
            right_ref[p, c, STATE:, :] = scaled
            add = dot(keys_ref[c], scaled)
            if c == 0:
                right_ref[p, c, :STATE, :] = jnp.zeros((STATE, WIDE), BF16)
                state = rows[16 + c : 17 + c] * add
            else:
                faded = rows[c : c + 1] * state
                right_ref[p, c, :STATE, :] = faded.astype(BF16)
                state = rows[32 + c : 33 + c] * faded + rows[16 + c : 17 + c] * add
        l_send[p] = state.astype(BF16).reshape(4, 32, WIDE)

    def to_quad(p, i):
        return pltpu.make_async_remote_copy(
            l_send.at[p, (member + i) % 4],
            q_recv.at[p, member],
            s1.at[p, i],
            r1.at[p, i],
            device_id={"slot": quad_peer(i)},
            device_id_type=MESH,
        )

    def owner_of(p, tile):
        return 4 * tile + (p + 4 - tile) % 4

    def to_owner(p, tile):
        return pltpu.make_async_remote_copy(
            t_send.at[p, tile],
            o_recv.at[quad],
            s2.at[p, tile],
            r2.at[quad],
            device_id={"slot": owner_of(p, tile) * 4 + member},
            device_id_type=MESH,
        )

    my_part = (quad // 4 + quad % 4) % 4
    my_tile = quad // 4

    def from_owner(i):
        return pltpu.make_async_remote_copy(
            o_send.at[(quad + i) % QUADS],
            g_recv.at[my_part, my_tile],
            s3.at[i],
            r3.at[my_part, my_tile],
            device_id={"slot": far_peer(i)},
            device_id_type=MESH,
        )

    def to_member(p, i):
        return pltpu.make_async_remote_copy(
            p_send.at[p, (member + i) % 4],
            c_recv.at[p, member],
            s4.at[p, i],
            r4.at[p, i],
            device_id={"slot": quad_peer(i)},
            device_id_type=MESH,
        )

    def decay_of(p, i):
        row = pl.ds(quad * 4 + i, 1)
        return jnp.concatenate([decay_wide[2 * p, row, :], decay_wide[2 * p + 1, row, :]], axis=1)

    def quad_totals(p):
        for i in range(1, 4):
            to_quad(p, i).wait_recv()
        run = q_recv[p, 0].astype(F32)
        for i in range(1, 4):
            run = decay_of(p, i) * run + q_recv[p, i].astype(F32)
        run = run.astype(BF16)
        for tile in range(4):
            r, l = tile // 2, tile % 2
            t_send[p, tile] = run[16 * r : 16 * r + 16, 128 * l : 128 * l + 128]
        for tile in range(4):
            mine = owner_of(p, tile) == quad

            @pl.when(mine)
            def _():
                o_recv[quad] = t_send[p, tile]

            @pl.when(jnp.logical_not(mine))
            def _():
                to_owner(p, tile).start()

    def own():
        def wait_one(i, c):
            source = (quad + i) % QUADS
            pltpu.make_async_remote_copy(
                t_send.at[0, 0],
                o_recv.at[source],
                s2.at[0, 0],
                r2.at[source],
                device_id={"slot": far_peer(i)},
                device_id_type=MESH,
            ).wait_recv()
            return c

        lax.fori_loop(1, QUADS, wait_one, 0)
        tile = 2 * my_part + my_tile % 2
        run = jnp.zeros((16, 128), F32)
        for q in range(QUADS):
            o_send[q] = run.astype(BF16)
            fade = decay_wide[tile, 4 * q : 4 * q + 1, :]
            for i in range(1, 4):
                fade = fade * decay_wide[tile, 4 * q + i : 4 * q + i + 1, :]
            run = fade * run + o_recv[q].astype(F32)
        g_recv[my_part, my_tile] = o_send[quad]
        lax.fori_loop(1, QUADS, lambda i, c: (from_owner(i).start(), c)[1], 0)

    def members(p):
        for tile in range(4):

            @pl.when(owner_of(p, tile) != quad)
            def _():
                pltpu.make_async_remote_copy(
                    o_send.at[0],
                    g_recv.at[p, tile],
                    s3.at[0],
                    r3.at[p, tile],
                    device_id={"slot": after},
                    device_id_type=MESH,
                ).wait_recv()

        tiles = [g_recv[p, tile].astype(F32) for tile in range(4)]
        run = jnp.concatenate(
            [
                jnp.concatenate([tiles[0], tiles[1]], axis=1),
                jnp.concatenate([tiles[2], tiles[3]], axis=1),
            ],
            axis=0,
        )
        for i in range(4):
            p_send[p, i] = run.astype(BF16)
            if i < 3:
                run = decay_of(p, i) * run + q_recv[p, i].astype(F32)
        c_recv[p, member] = p_send[p, member]
        for i in range(1, 4):
            to_member(p, i).start()

    def local(p):
        z_copy(p).wait()
        matrix = widen_matrix(p, 32)
        skip_row = dot(rows_ref[48:64, :], matrix)[0:1]
        for c in range(subs):
            at = slice(c * SUB, (c + 1) * SUB)
            y = dot(left_ref[c], right_ref[p, c]) * dot(e_ref[at, :], matrix)
            y = y + skip_row * xconv[p, at, :].astype(F32)
            gate = silu(zs[p, at, :].astype(F32))
            y_ref[p, at, :] = y * gate
            g_ref[p, at, :] = dot(ef_ref[at, :], matrix) * gate

    def finish(p):
        for i in range(1, 4):
            to_member(p, i).wait_recv()
        carried = c_recv[p].reshape(STATE, WIDE)
        for c in range(subs):
            at = slice(c * SUB, (c + 1) * SUB)
            gated = y_ref[p, at, :] + g_ref[p, at, :] * dot(c_ref[at, :], carried)
            y_ref[p, at, :] = gated
            square = gated * gated
            sq_ref[at, :] += square[:, :128] + square[:, 128:]

    def first_pass(p, carry):
        states(p)
        for i in range(1, 4):
            to_quad(p, i).start()
        q_recv[p, member] = l_send[p, member]

        @pl.when(p == 0)
        def _():
            def wait_decay(i, c):
                source = ((quad + QUADS - i) % QUADS) * 4
                pltpu.make_async_remote_copy(
                    decay_all.at[pl.ds(source, 4)],
                    decay_all.at[pl.ds(source, 4)],
                    d_send2.at[i],
                    d_recv2.at[i],
                    device_id={"slot": far_peer(i)},
                    device_id_type=MESH,
                ).wait_recv()
                return c

            lax.fori_loop(1, QUADS, wait_decay, 0)
            for k in range(slots):
                decay_rows[k : k + 1, :] = decay_all[k]
            rest = decay_rows[...]
            wide = [jnp.zeros((slots, WIDE), F32) for _ in range(PARTS)]
            for _ in range(3):
                term = rest.astype(BF16)
                rest = rest - term.astype(F32)
                for q in range(PARTS):
                    r = iota((128, WIDE), 0)
                    matrix = (r == 4 * q + iota((128, WIDE), 1) // HEAD_DIM).astype(F32).astype(BF16)
                    wide[q] = wide[q] + dot(term, matrix)
            for q in range(PARTS):
                decay_wide[2 * q] = wide[q][:, :128]
                decay_wide[2 * q + 1] = wide[q][:, 128:]

        @pl.when(p >= 1)
        def _():
            quad_totals(p - 1)

        @pl.when((p >= 2) & (my_part == p - 2))
        def _():
            own()

        return carry

    def second_pass(p, carry):
        @pl.when(p == 0)
        def _():
            quad_totals(PARTS - 1)

        @pl.when((p < 2) & (my_part == p + 2))
        def _():
            own()

        local(p)

        @pl.when(p >= 1)
        def _():
            members(p - 1)

        return carry

    lax.fori_loop(0, PARTS, first_pass, 0)
    lax.fori_loop(0, PARTS, second_pass, 0)
    members(PARTS - 1)
    sq_ref[...] = jnp.zeros_like(sq_ref)
    lax.fori_loop(0, PARTS, lambda p, c: (finish(p), c)[1], 0)

    sums = exact_dot(jnp.ones((8, 128), F32), sq_ref[...], ((1,), (1,)))
    n_send[0] = sums[0:1]
    n_recv[tp] = sums[0:1]

    def to_tp(i):
        return pltpu.make_async_remote_copy(
            n_send.at[0],
            n_recv.at[tp],
            ns.at[i],
            nr.at[i],
            device_id={"tp": (tp + i) % tp_size},
            device_id_type=MESH,
        )

    for i in range(1, tp_size):
        to_tp(i).start()
    for i in range(1, tp_size):
        to_tp(i).wait_recv()
    n_rows[...] = jnp.zeros_like(n_rows)
    for k in range(tp_size):
        n_rows[k : k + 1, :] = n_recv[k]
    everyone = exact_dot(n_rows[...], jnp.ones((8, 128), F32), ((0,), (0,)))
    sq_ref[...] = lax.rsqrt(everyone * (1.0 / (PARTS * WIDE * tp_size)) + EPSILON)

    def out_copy(p):
        return pltpu.make_async_copy(
            o_ref.at[p], out_hbm.at[:, pl.ds(p * WIDE, WIDE)], out_sem.at[p]
        )

    def write(p, carry):
        gain = norm_ref[p]
        for c in range(subs):
            at = slice(c * SUB, (c + 1) * SUB)
            scale = sq_ref[at, :]
            scale = jnp.concatenate([scale, scale], axis=1)
            o_ref[p, at, :] = (y_ref[p, at, :] * scale * gain).astype(BF16)
        return carry

    for p in range(PARTS):
        write(p, 0)
        out_copy(p).start()

    for halo in halos:
        halo.wait_send()
    for i in range(1, 4):
        near_decay(i).wait_send()
    lax.fori_loop(1, QUADS, lambda i, c: (far_decay(i).wait_send(), c)[1], 0)
    for p in range(PARTS):
        for i in range(1, 4):
            to_quad(p, i).wait_send()
            to_member(p, i).wait_send()
        for tile in range(4):

            @pl.when(owner_of(p, tile) != quad)
            def _():
                to_owner(p, tile).wait_send()

    lax.fori_loop(1, QUADS, lambda i, c: (from_owner(i).wait_send(), c)[1], 0)
    for i in range(1, tp_size):
        to_tp(i).wait_send()
    for p in range(PARTS):
        out_copy(p).wait()


def body(x_in, bc_in, z_gate, decay_rate, step_size, d_skip, conv_x, conv_bc, norm_weight, lengths):
    tokens, columns = x_in.shape
    subs = tokens // SUB
    tp_size = lax.axis_size("tp")
    heads = columns // HEAD_DIM
    vmem = pl.BlockSpec(memory_space=pltpu.VMEM)
    hbm = pl.BlockSpec(memory_space=pl.ANY)
    dma = pltpu.SemaphoreType.DMA
    split_taps = conv_x.reshape(4, PARTS, WIDE).transpose(1, 0, 2)
    return pl.pallas_call(
        functools.partial(kernel, tp_size),
        out_shape=jax.ShapeDtypeStruct((tokens, columns), BF16),
        in_specs=[pl.BlockSpec(memory_space=pltpu.SMEM), hbm, vmem, hbm] + [vmem] * 6,
        out_specs=hbm,
        scratch_shapes=[
            pltpu.VMEM((PARTS, 16 + tokens, WIDE), BF16),
            pltpu.VMEM((PARTS, tokens, WIDE), BF16),
            pltpu.VMEM((16 + tokens, 2 * STATE), BF16),
            pltpu.VMEM((subs, 3 * SUB, 80), BF16),
            pltpu.VMEM((subs, SUB, STATE + SUB), BF16),
            pltpu.VMEM((PARTS, subs, STATE + SUB, WIDE), BF16),
            pltpu.VMEM((subs, STATE, SUB), BF16),
            pltpu.VMEM((tokens, STATE), BF16),
            pltpu.VMEM((PARTS, tokens, WIDE), BF16),
            pltpu.VMEM((tokens, 32), F32),
            pltpu.VMEM((16, 32), F32),
            pltpu.VMEM((16, 32), F32),
            pltpu.VMEM((tokens, 32), BF16),
            pltpu.VMEM((tokens, 32), BF16),
            pltpu.VMEM((tokens, 32), BF16),
            pltpu.VMEM((64, 32), BF16),
            pltpu.VMEM((PARTS, tokens, WIDE), F32),
            pltpu.VMEM((PARTS, tokens, WIDE), F32),
            pltpu.VMEM((tokens, 128), F32),
            pltpu.VMEM((PARTS, tokens, WIDE), BF16),
            pltpu.VMEM((4 * QUADS, 1, 128), F32),
            pltpu.VMEM((4 * QUADS, 128), F32),
            pltpu.VMEM((8, 4 * QUADS, 128), F32),
            pltpu.VMEM((PARTS, 4, 32, WIDE), BF16),
            pltpu.VMEM((PARTS, 4, 32, WIDE), BF16),
            pltpu.VMEM((PARTS, 4, 16, 128), BF16),
            pltpu.VMEM((QUADS, 16, 128), BF16),
            pltpu.VMEM((QUADS, 16, 128), BF16),
            pltpu.VMEM((PARTS, 4, 16, 128), BF16),
            pltpu.VMEM((PARTS, 4, 32, WIDE), BF16),
            pltpu.VMEM((PARTS, 4, 32, WIDE), BF16),
            pltpu.VMEM((1, 1, tokens), F32),
            pltpu.VMEM((tp_size, 1, tokens), F32),
            pltpu.VMEM((8, tokens), F32),
            dma((2 * PARTS,)),
            dma((PARTS,)),
            dma((PARTS + 1,)),
            dma((PARTS + 1,)),
            dma((4,)),
            dma((4,)),
            dma((QUADS,)),
            dma((QUADS,)),
            dma((PARTS, 4)),
            dma((PARTS, 4)),
            dma((PARTS, 4)),
            dma((QUADS,)),
            dma((QUADS,)),
            dma((PARTS, 4)),
            dma((PARTS, 4)),
            dma((PARTS, 4)),
            dma((tp_size,)),
            dma((tp_size,)),
        ],
        compiler_params=pltpu.CompilerParams(
            collective_id=0, has_side_effects=True, vmem_limit_bytes=56 * 1024 * 1024
        ),
    )(
        lengths,
        x_in,
        bc_in,
        z_gate,
        decay_rate,
        step_size,
        d_skip.reshape(1, heads),
        split_taps,
        conv_bc,
        norm_weight.reshape(PARTS, 1, WIDE),
    )


def solution(mesh):
    placed = (
        P("slot", "tp"),
        P("slot", "tp"),
        P("slot", "tp"),
        P("slot", "tp"),
        P("slot", "tp"),
        P("tp"),
        P(None, "tp"),
        P(None, "tp"),
        P("tp"),
        P(),
    )
    return jax.shard_map(
        body, mesh=mesh, in_specs=placed, out_specs=P("slot", "tp"), check_vma=False
    )
```

time: 444 us -> 85.6 us (0.19)
  waiting for transfers between devices: 170 us -> 0 us
  other arithmetic: 96.4 us -> 0 us
  blocking collectives: 83 us -> 0 us
  Pallas kernels: 0 us -> 79.2 us
  matrix products: 37.1 us -> 0 us
  local copies, waits for them, and re-layouts: 24.6 us -> 6.09 us
  between operations: 13.6 us -> 0.01 us
  starting transfers between devices: 7.92 us -> 0 us
  loops' own time: 7.46 us -> 0 us
    all_gather x1 -> x0, waiting for transfers between devices: 170 us -> none  [carried_in(): everything = jax.tree.map(lambda part: lax.all_gather(part, axis), array)]
    pallas_call x0 -> x1, Pallas kernels: none -> 79.2 us  [body(): pl.pallas_call(functools.partial(kernel, tp_size), out_shape=jax.ShapeDty...]
    select_n x65 -> x0, other arithmetic: 75.9 us -> none  [the longest x64 75 us: step(): return jax.tree.map(lambda a, b: jnp.where(reached, a, b), new, before)]
    all_gather x1 -> x0, blocking collectives: 70.1 us -> none  [carried_in(): everything = jax.tree.map(lambda part: lax.all_gather(part, axis), array)]
    dot_general x11 -> x0, matrix products: 37.1 us -> none  [the longest x8 33.2 us: pair_fn(): jnp.einsum('hts,shp->thp', weights, pair_vals, preferred_element_type=jnp...]
    psum x1 -> x0, blocking collectives: 12.9 us -> none  [body(): total_sq = lax.psum(jnp.sum(gated_rows * gated_rows, axis=1), 'tp')]
    ppermute x2 -> x0, starting transfers between devices: 7.91 us -> none  [from_behind(): return lax.ppermute(block, axis, route)]
    another operation x2 -> x0, loops' own time: 7.46 us -> none  [the longest x1 5.23 us: span_terms(): y_pairs = lax.map(pair_fn, jnp.arange(head_count // 2, dtype=jnp.int32))]
  transfers between devices with their start and end apart: 3 -> 0, of which waited for: 1 -> 0; matrix products, arithmetic and copies ran while one was open for 15% -> 0% of each run, Pallas kernels for 0% -> 0%
where the time goes in v1:
time: 85.6 us; the launch traced here: 85.3 us
  Pallas kernels  79.2 us (93%)
  local copies, waits for them, and re-layouts  6.09 us (7%)
    pallas_call x1, Pallas kernels, body(): pl.pallas_call(functools.partial(kernel, tp_size), out_shape=jax.ShapeDty...  79.2 us
    unnamed x3, local copies, waits for them, and re-layouts  6.09 us

profile of v1, /device:TPU:1, one launch (start us, length us, event | category | flops | bytes accessed | tf_op | source)
XLA Modules:
  0.0 85.3 jit_solution(8604729974511954246)
XLA Ops:
  0.0 1.7 %copy.11.rate_ref = f32[768,16]{1,0:T(8,128)} copy(f32[768,16]{0,1:T(8,128)} %param.13) | data formatting | bytes 98304 | tf_op args[3]
  1.7 1.7 %copy.12.step_ref = f32[768,16]{1,0:T(8,128)} copy(f32[768,16]{0,1:T(8,128)} %param.14) | data formatting | bytes 98304 | tf_op args[4]
  3.4 79.2 %shard_map.100 = bf16[768,1024]{1,0:T(8,128)(2,1)} custom-call(s32[4]{0:T(128)} %len_ref.1, bf16[768,1024]{1,0:T(8,128)(2,1)} %x_hbm.1, bf16[768,256]{1,0:T(8,128)(2,1)} %bc_ref.1, bf16[768,1024]{1,0:T(8,128)(2,1)} %z_hbm.1, f32[768,16]{1,0:T(8,128)} %copy.11.rate_ref, f32[768,16]{1,0:T(8,128)} %copy.12.step_ref, f32[1,16]{1,0:T(1,128)} %bitcast.7, ...), custom_call_target="tpu_custom_call" | custom-call | tf_op jit(solution)/shard_map/pallas_call | solution.py:628
  82.6 2.7 %copy.14 = bf16[768,1024]{1,0:T(8,128)(2,1)} copy(bf16[768,1024]{1,0:T(8,128)(2,1)} %shard_map.100) | data formatting | bytes 3145728

commit v2 on v1

--- a/solution.py
+++ b/solution.py
@@ -54,31 +54,38 @@
     skip_ref,
     conv_x_ref,
     conv_bc_ref,
-    norm_ref,
-    out_hbm,
+    y_ref,
+    sq_ref,
     xs,
     zs,
+    x_edge,
+    bc_edge,
+    bc0_ref,
     bcs,
     shift_ref,
+    group_ref,
     left_ref,
     right_ref,
-    keys_ref,
     c_ref,
     xconv,
     cum_ref,
+    st_ref,
+    u_ref,
+    e_send,
+    e_recv,
+    e_rows,
+    n_state,
     mid_ref,
     end_ref,
     f_ref,
     e_ref,
     ef_ref,
     rows_ref,
-    y_ref,
     g_ref,
-    sq_ref,
-    o_ref,
     decay_all,
     decay_rows,
     decay_wide,
+    decay_near,
     l_send,
     q_recv,
     t_send,
@@ -89,11 +96,11 @@
     c_recv,
     n_send,
     n_recv,
-    n_rows,
     in_sem,
-    out_sem,
     halo_send,
     halo_recv,
+    edge_send,
+    edge_recv,
     d_send1,
     d_recv1,
     d_send2,
@@ -140,11 +147,11 @@
     def greet(peer):
         pl.semaphore_signal(barrier, inc=1, device_id={"slot": peer}, device_id_type=MESH)
 
+    lax.fori_loop(1, QUADS, lambda i, c: (greet(far_peer(i)), c)[1], 0)
+    for i in range(1, 4):
+        greet(quad_peer(i))
     greet(after)
     greet(before)
-    for i in range(1, 4):
-        greet(quad_peer(i))
-    lax.fori_loop(1, QUADS, lambda i, c: (greet(far_peer(i)), c)[1], 0)
     for i in range(1, tp_size):
         pl.semaphore_signal(
             barrier, inc=1, device_id={"tp": (tp + i) % tp_size}, device_id_type=MESH
@@ -166,16 +173,17 @@
             start = jnp.where(pos >= end, end, start)
         return start
 
-    twice = (iota((16, 32), 0) == iota((16, 32), 1) % 16).astype(F32)
     zero_one = iota((128, 128), 0), iota((128, 128), 1)
     tri = ((zero_one[0] >= zero_one[1]) & (zero_one[0] // SUB == zero_one[1] // SUB)).astype(F32)
     width = min(128, tokens)
+    eye = (zero_one[0] == zero_one[1]).astype(F32)
     for b in range(tokens // width):
-        rate = rate_ref[b * width : (b + 1) * width, :]
-        rate = jnp.concatenate([rate, rate], axis=1)
-        cum_ref[b * width : (b + 1) * width, :] = exact_dot(
-            tri[:width, :width], rate, ((1,), (0,))
-        )
+        at = slice(b * width, (b + 1) * width)
+        rate, step = rate_ref[:, at], step_ref[:, at]
+        rate = jnp.concatenate([rate, rate], axis=0)
+        step = jnp.concatenate([step, step], axis=0)
+        cum_ref[at, :] = exact_dot(tri[:width, :width], rate, ((1,), (1,)))
+        st_ref[at, :] = exact_dot(eye[:width, :width], step, ((1,), (1,)))
     mid_ref[...] = jnp.zeros_like(mid_ref)
     end_ref[...] = jnp.zeros_like(end_ref)
     offset = jnp.zeros((1, 32), F32)
@@ -186,9 +194,7 @@
         end = cum_ref[c * SUB + 63 : c * SUB + 64, :]
         mid_ref[c : c + 1, :] = mid
         end_ref[c : c + 1, :] = end
-        step = step_ref[at, :]
-        step = jnp.concatenate([step, step], axis=1)
-        f_ref[at, :] = two_terms(jnp.exp(cum - mid) * step)
+        f_ref[at, :] = two_terms(jnp.exp(cum - mid) * st_ref[at, :])
         e_ref[at, :] = two_terms(jnp.exp(mid - cum))
         pos = first_row + c * SUB + iota((SUB, 32), 0)
         open_rows = start_of(pos, ends[:3]) < first_row
@@ -211,79 +217,43 @@
         jnp.broadcast_to(jnp.concatenate([skip, skip], axis=1), (16, 32))
     )
 
-    for c in range(subs):
-        base = first_row + c * SUB
-        t = iota((SUB, 80), 0)
-        s = iota((SUB, 80), 1) - 16
-        inside = (base + s) >= start_of(base + t, ends)
-        for d in range(1, 4):
-            shift_ref[c, (d - 1) * SUB : d * SUB, :] = ((s == t - d) & inside).astype(F32).astype(BF16)
-
-    pl.semaphore_wait(barrier, 2 + 3 + (QUADS - 1) + (tp_size - 1))
-    halos = []
-    for p in range(PARTS):
-        halos.append(
-            pltpu.make_async_remote_copy(
-                x_hbm.at[pl.ds(tokens - 16, 16), pl.ds(p * WIDE, WIDE)],
-                xs.at[p, pl.ds(0, 16)],
-                halo_send.at[p],
-                halo_recv.at[p],
-                device_id={"slot": after},
-                device_id_type=MESH,
-            )
-        )
-    halos.append(
-        pltpu.make_async_remote_copy(
-            bc_ref.at[pl.ds(tokens - 16, 16)],
-            bcs.at[pl.ds(0, 16)],
-            halo_send.at[PARTS],
-            halo_recv.at[PARTS],
-            device_id={"slot": after},
-            device_id_type=MESH,
-        )
-    )
-    halos[PARTS].start()
-    for p in range(PARTS):
-        halos[p].start()
-
-    def near_decay(i):
-        return pltpu.make_async_remote_copy(
-            decay_all.at[slot],
-            decay_all.at[slot],
-            d_send1.at[i],
-            d_recv1.at[i],
-            device_id={"slot": quad_peer(i)},
-            device_id_type=MESH,
-        )
-
-    def far_decay(i):
-        return pltpu.make_async_remote_copy(
-            decay_all.at[pl.ds(quad * 4, 4)],
-            decay_all.at[pl.ds(quad * 4, 4)],
-            d_send2.at[i],
-            d_recv2.at[i],
-            device_id={"slot": far_peer(i)},
-            device_id_type=MESH,
-        )
-
-    for i in range(1, 4):
-        near_decay(i).start()
-
+    blocks = [(row, min(192, tokens - row)) for row in range(0, tokens, 192)]
+
+    def shifts_at(row, count):
+        t = iota((count, count + 16), 0)
+        s = iota((count, count + 16), 1) - 16
+        inside = (first_row + row + s) >= start_of(first_row + row + t, ends)
+        return [((s == t - d) & inside).astype(F32).astype(BF16) for d in range(1, 4)]
+
+    for k, (row, count) in enumerate(blocks):
+        for d, one in enumerate(shifts_at(row, count)):
+            shift_ref[k, d * count : (d + 1) * count, : count + 16] = one
+
+    bcs[:16, :] = jnp.zeros((16, 2 * STATE), BF16)
     bcs[16:, :] = bc_ref[...]
-    halos[PARTS].wait_recv()
+    for p in range(PARTS):
+        xs[p, :16, :] = jnp.zeros((16, WIDE), BF16)
 
     def conv(rows, shifts, taps):
         moved = dot(shifts, rows)
+        count = rows.shape[0] - 16
         summed = taps[3:4] * rows[16:].astype(F32)
         for d in range(1, 4):
-            summed = summed + taps[3 - d : 4 - d] * moved[(d - 1) * SUB : d * SUB]
+            summed = summed + taps[3 - d : 4 - d] * moved[(d - 1) * count : d * count]
         return silu(summed).astype(BF16)
 
-    for c in range(subs):
+    def block_shifts(k):
+        count = blocks[k][1]
+        return shift_ref[k, : 3 * count, : count + 16]
+
+    groups = [(c, min(4, subs - c)) for c in range(0, subs, 4)]
+
+    def keys_and_queries(c, bc, again=False):
         base = first_row + c * SUB
-        bc = conv(bcs[c * SUB : c * SUB + 80, :], shift_ref[c], conv_bc_ref[...])
         key, query = bc[:, :STATE], bc[:, STATE:]
         c_ref[c * SUB : (c + 1) * SUB, :] = query
+        if c == 0:
+            bc0_ref[...] = bc
         scores = lax.dot_general(query, key, (((1,), (1,)), ((), ())), preferred_element_type=F32)
         t = iota((SUB, SUB), 0)
         s = iota((SUB, SUB), 1)
@@ -294,45 +264,137 @@
         left_ref[c, :, :STATE] = jnp.where(from_before, query.astype(F32), 0.0).astype(BF16)
         last = start_of(jnp.zeros((SUB, STATE), jnp.int32) + (base + SUB - 1), ends)
         keys = jnp.where(row >= last, key.astype(F32), 0.0)
-        keys_ref[c] = keys.T.astype(BF16)
-
-    for i in range(1, 4):
-        near_decay(i).wait_recv()
-    lax.fori_loop(1, QUADS, lambda i, c: (far_decay(i).start(), c)[1], 0)
+        if not again:
+            g, i = c // 4, c % 4
+            group_ref[g, i * STATE : (i + 1) * STATE, i * SUB : (i + 1) * SUB] = keys.T.astype(BF16)
+
+    group_ref[...] = jnp.zeros_like(group_ref)
+    for k, (row, count) in enumerate(blocks):
+        bc = conv(bcs[row : row + count + 16, :], block_shifts(k), conv_bc_ref[...])
+        for i in range(count // SUB):
+            keys_and_queries(row // SUB + i, bc[i * SUB : (i + 1) * SUB])
 
     def widen_matrix(p, rows):
         r = iota((rows, WIDE), 0) % 16
         return (r == 4 * p + iota((rows, WIDE), 1) // HEAD_DIM).astype(F32).astype(BF16)
 
-    def states(p):
+    def row_factors(p):
+        return dot(rows_ref[...], widen_matrix(p, 32))
+
+    def later_subs(p, carry):
         x_copy(p).wait()
-        pltpu.make_async_remote_copy(
-            x_hbm.at[pl.ds(tokens - 16, 16), pl.ds(0, WIDE)],
-            xs.at[p, pl.ds(0, 16)],
-            halo_send.at[p],
-            halo_recv.at[p],
-            device_id={"slot": after},
-            device_id_type=MESH,
-        ).wait_recv()
         taps = conv_x_ref[p]
-        matrix = widen_matrix(p, 32)
-        rows = dot(rows_ref[...], matrix)
+        wide_f = dot(f_ref[...], widen_matrix(p, 32))
+        rows = row_factors(p)
+        parts = []
+        for k, (row, count) in enumerate(blocks):
+            values = conv(xs[p, row : row + count + 16, :], block_shifts(k), taps)
+            xconv[p, row : row + count, :] = values
+            scaled = values.astype(F32) * wide_f[row : row + count]
+            if row == 0:
+                scaled = jnp.where(iota(scaled.shape, 0) >= 3, scaled, 0.0)
+            scaled = scaled.astype(BF16)
+            for i in range(count // SUB):
+                one = scaled[i * SUB : (i + 1) * SUB]
+                right_ref[p, row // SUB + i, STATE:, :] = one
+                parts.append(one)
         state = jnp.zeros((STATE, WIDE), F32)
-        for c in range(subs):
-            at = slice(c * SUB, (c + 1) * SUB)
-            values = conv(xs[p, c * SUB : c * SUB + 80, :], shift_ref[c], taps)
-            xconv[p, at, :] = values
-            scaled = (values.astype(F32) * dot(f_ref[at, :], matrix)).astype(BF16)
-            right_ref[p, c, STATE:, :] = scaled
-            add = dot(keys_ref[c], scaled)
-            if c == 0:
-                right_ref[p, c, :STATE, :] = jnp.zeros((STATE, WIDE), BF16)
-                state = rows[16 + c : 17 + c] * add
-            else:
-                faded = rows[c : c + 1] * state
-                right_ref[p, c, :STATE, :] = faded.astype(BF16)
-                state = rows[32 + c : 33 + c] * faded + rows[16 + c : 17 + c] * add
+        for g, (first, many) in enumerate(groups):
+            scaled = jnp.concatenate(parts[first : first + many], axis=0)
+            adds = dot(group_ref[g, : many * STATE, : many * SUB], scaled)
+            for i in range(many):
+                c = first + i
+                add = adds[i * STATE : (i + 1) * STATE]
+                u_ref[p, c] = add
+                if c == 0:
+                    state = rows[16:17] * add
+                else:
+                    state = rows[32 + c : 33 + c] * rows[c : c + 1] * state + rows[16 + c : 17 + c] * add
         l_send[p] = state.astype(BF16).reshape(4, 32, WIDE)
+        q_recv[p, member] = l_send[p, member]
+        return carry
+
+    def edge_fade(rows):
+        fade = rows[16:17]
+        for c in range(1, subs):
+            fade = fade * rows[32 + c : 33 + c] * rows[c : c + 1]
+        return fade
+
+    edge_shape = (16, STATE)
+
+    def edge():
+        shifts = jnp.concatenate(shifts_at(0, 16), axis=0)
+        halos[PARTS].wait_recv()
+        bc = conv(bc_edge[...], shifts, conv_bc_ref[...])
+        bc0_ref[0:16, :] = bc
+        row = first_row + iota(edge_shape, 0)
+        last = start_of(jnp.zeros(edge_shape, jnp.int32) + (first_row + SUB - 1), ends)
+        keys = jnp.where(row >= last, bc[:, :STATE].astype(F32), 0.0)
+        for t in range(3):
+            e_send[t, :, PARTS * WIDE :] = keys[t : t + 1]
+        for p in range(PARTS):
+            halos[p].wait_recv()
+        every = range(PARTS)
+        rows = [row_factors(p) for p in every]
+        wide_f = [dot(f_ref[0:16, :], widen_matrix(p, 32)) for p in every]
+        values = [conv(x_edge[p], shifts, conv_x_ref[p]) for p in every]
+        scaled = [(values[p].astype(F32) * wide_f[p]).astype(BF16) for p in every]
+        for p in every:
+            faded = scaled[p].astype(F32) * edge_fade(rows[p])
+            for t in range(3):
+                e_send[t, :, p * WIDE : (p + 1) * WIDE] = faded[t : t + 1]
+        for i in range(1, 4):
+            edge_to(i).start()
+        first_three = jnp.where(iota(edge_shape, 0) < 3, keys, 0.0).astype(BF16)
+        for p in every:
+            xconv[p, 0:16, :] = values[p]
+            right_ref[p, 0, STATE : STATE + 16, :] = scaled[p]
+            u_ref[p, 0] += lax.dot_general(
+                first_three, scaled[p], (((0,), (0,)), ((), ())), preferred_element_type=F32
+            )
+        keys_and_queries(0, bc0_ref[...], again=True)
+
+    def edge_to(i):
+        return pltpu.make_async_remote_copy(
+            e_send,
+            e_recv.at[pl.ds(member * 3, 3)],
+            edge_send.at[i],
+            edge_recv.at[i],
+            device_id={"slot": quad_peer(i)},
+            device_id_type=MESH,
+        )
+
+    def edge_rows():
+        for i in range(1, 4):
+            edge_to(i).wait_recv()
+        for t in range(3):
+            e_recv[member * 3 + t] = e_send[t]
+        e_rows[...] = jnp.zeros_like(e_rows)
+        for i in range(4):
+            for t in range(3):
+                e_rows[i, t : t + 1, :] = e_recv[i * 3 + t]
+
+    def quad_state(p, i):
+        pick = (iota((32, STATE), 1) == member * 32 + iota((32, STATE), 0)).astype(F32).astype(BF16)
+        keys = e_rows[i, :, PARTS * WIDE :].astype(BF16)
+        keys = lax.dot_general(pick, keys, (((1,), (1,)), ((), ())), preferred_element_type=F32)
+        values = e_rows[i, :, p * WIDE : (p + 1) * WIDE].astype(BF16)
+        return q_recv[p, i].astype(F32) + dot(keys.astype(BF16), values)
+
+    def chain(p):
+        rows = row_factors(p)
+        right_ref[p, 0, :STATE, :] = jnp.zeros((STATE, WIDE), BF16)
+        state = rows[16:17] * u_ref[p, 0]
+        for c in range(1, subs):
+            faded = rows[c : c + 1] * state
+            right_ref[p, c, :STATE, :] = faded.astype(BF16)
+            if c + 1 < subs:
+                state = rows[32 + c : 33 + c] * faded + rows[16 + c : 17 + c] * u_ref[p, c]
+
+    lax.fori_loop(0, PARTS, later_subs, 0)
+    for p in range(PARTS):
+        x_edge[p, 16:, :] = xs[p, 16:32, :]
+    bc_edge[16:, :] = bc_ref[:16, :]
 
     def to_quad(p, i):
         return pltpu.make_async_remote_copy(
@@ -344,6 +406,60 @@
             device_id_type=MESH,
         )
 
+    pl.semaphore_wait(barrier, 2 + 3 + (QUADS - 1) + (tp_size - 1))
+    halos = []
+    for p in range(PARTS):
+        halos.append(
+            pltpu.make_async_remote_copy(
+                x_hbm.at[pl.ds(tokens - 16, 16), pl.ds(p * WIDE, WIDE)],
+                x_edge.at[p, pl.ds(0, 16)],
+                halo_send.at[p],
+                halo_recv.at[p],
+                device_id={"slot": after},
+                device_id_type=MESH,
+            )
+        )
+    halos.append(
+        pltpu.make_async_remote_copy(
+            bc_ref.at[pl.ds(tokens - 16, 16)],
+            bc_edge.at[pl.ds(0, 16)],
+            halo_send.at[PARTS],
+            halo_recv.at[PARTS],
+            device_id={"slot": after},
+            device_id_type=MESH,
+        )
+    )
+    halos[PARTS].start()
+    for p in range(PARTS):
+        halos[p].start()
+
+    def near_decay(i):
+        return pltpu.make_async_remote_copy(
+            decay_all.at[slot],
+            decay_all.at[slot],
+            d_send1.at[i],
+            d_recv1.at[i],
+            device_id={"slot": quad_peer(i)},
+            device_id_type=MESH,
+        )
+
+    def far_decay(i):
+        return pltpu.make_async_remote_copy(
+            decay_all.at[pl.ds(quad * 4, 4)],
+            decay_all.at[pl.ds(quad * 4, 4)],
+            d_send2.at[i],
+            d_recv2.at[i],
+            device_id={"slot": far_peer(i)},
+            device_id_type=MESH,
+        )
+
+    for p in range(PARTS):
+        for i in range(1, 4):
+            to_quad(p, i).start()
+    for i in range(1, 4):
+        near_decay(i).start()
+
+
     def owner_of(p, tile):
         return 4 * tile + (p + 4 - tile) % 4
 
@@ -381,15 +497,17 @@
         )
 
     def decay_of(p, i):
-        row = pl.ds(quad * 4 + i, 1)
-        return jnp.concatenate([decay_wide[2 * p, row, :], decay_wide[2 * p + 1, row, :]], axis=1)
+        return decay_near[p, i : i + 1, :]
 
     def quad_totals(p):
         for i in range(1, 4):
             to_quad(p, i).wait_recv()
-        run = q_recv[p, 0].astype(F32)
+        run = quad_state(p, 0)
+        n_state[p, 0] = run
         for i in range(1, 4):
-            run = decay_of(p, i) * run + q_recv[p, i].astype(F32)
+            new = quad_state(p, i)
+            n_state[p, i] = new
+            run = decay_of(p, i) * run + new
         run = run.astype(BF16)
         for tile in range(4):
             r, l = tile // 2, tile % 2
@@ -455,7 +573,7 @@
         for i in range(4):
             p_send[p, i] = run.astype(BF16)
             if i < 3:
-                run = decay_of(p, i) * run + q_recv[p, i].astype(F32)
+                run = decay_of(p, i) * run + n_state[p, i]
         c_recv[p, member] = p_send[p, member]
         for i in range(1, 4):
             to_member(p, i).start()
@@ -483,76 +601,74 @@
             square = gated * gated
             sq_ref[at, :] += square[:, :128] + square[:, 128:]
 
-    def first_pass(p, carry):
-        states(p)
-        for i in range(1, 4):
-            to_quad(p, i).start()
-        q_recv[p, member] = l_send[p, member]
-
-        @pl.when(p == 0)
-        def _():
-            def wait_decay(i, c):
-                source = ((quad + QUADS - i) % QUADS) * 4
-                pltpu.make_async_remote_copy(
-                    decay_all.at[pl.ds(source, 4)],
-                    decay_all.at[pl.ds(source, 4)],
-                    d_send2.at[i],
-                    d_recv2.at[i],
-                    device_id={"slot": far_peer(i)},
-                    device_id_type=MESH,
-                ).wait_recv()
-                return c
-
-            lax.fori_loop(1, QUADS, wait_decay, 0)
-            for k in range(slots):
-                decay_rows[k : k + 1, :] = decay_all[k]
-            rest = decay_rows[...]
-            wide = [jnp.zeros((slots, WIDE), F32) for _ in range(PARTS)]
-            for _ in range(3):
-                term = rest.astype(BF16)
-                rest = rest - term.astype(F32)
-                for q in range(PARTS):
-                    r = iota((128, WIDE), 0)
-                    matrix = (r == 4 * q + iota((128, WIDE), 1) // HEAD_DIM).astype(F32).astype(BF16)
-                    wide[q] = wide[q] + dot(term, matrix)
-            for q in range(PARTS):
-                decay_wide[2 * q] = wide[q][:, :128]
-                decay_wide[2 * q + 1] = wide[q][:, 128:]
-
-        @pl.when(p >= 1)
-        def _():
-            quad_totals(p - 1)
-
-        @pl.when((p >= 2) & (my_part == p - 2))
-        def _():
-            own()
-
+    def second_pass(p, carry):
+        chain(p)
+        local(p)
         return carry
 
-    def second_pass(p, carry):
-        @pl.when(p == 0)
-        def _():
-            quad_totals(PARTS - 1)
-
-        @pl.when((p < 2) & (my_part == p + 2))
-        def _():
-            own()
-
-        local(p)
-
-        @pl.when(p >= 1)
-        def _():
-            members(p - 1)
-
-        return carry
-
-    lax.fori_loop(0, PARTS, first_pass, 0)
-    lax.fori_loop(0, PARTS, second_pass, 0)
-    members(PARTS - 1)
+    edge()
+    lax.fori_loop(0, 2, second_pass, 0)
+    for i in range(1, 4):
+        near_decay(i).wait_recv()
+    lax.fori_loop(1, QUADS, lambda i, c: (far_decay(i).start(), c)[1], 0)
+    near = jnp.zeros((8, 128), F32)
+    for i in range(4):
+        near = jnp.where(iota((8, 128), 0) == i, decay_all[quad * 4 + i], near)
+    for p in range(PARTS):
+        rest = near
+        wide = jnp.zeros((8, WIDE), F32)
+        r = iota((128, WIDE), 0)
+        matrix = (r == 4 * p + iota((128, WIDE), 1) // HEAD_DIM).astype(F32).astype(BF16)
+        for _ in range(3):
+            term = rest.astype(BF16)
+            rest = rest - term.astype(F32)
+            wide = wide + dot(term, matrix)
+        decay_near[p] = wide
+    edge_rows()
+    for p in range(PARTS):
+        quad_totals(p)
+    lax.fori_loop(2, PARTS, second_pass, 0)
+
+    def wait_decay(i, c):
+        source = ((quad + QUADS - i) % QUADS) * 4
+        pltpu.make_async_remote_copy(
+            decay_all.at[pl.ds(source, 4)],
+            decay_all.at[pl.ds(source, 4)],
+            d_send2.at[i],
+            d_recv2.at[i],
+            device_id={"slot": far_peer(i)},
+            device_id_type=MESH,
+        ).wait_recv()
+        return c
+
+    lax.fori_loop(1, QUADS, wait_decay, 0)
+    for k in range(slots):
+        decay_rows[k : k + 1, :] = decay_all[k]
+    rest = decay_rows[...]
+    wide = [jnp.zeros((slots, WIDE), F32) for _ in range(PARTS)]
+    for _ in range(3):
+        term = rest.astype(BF16)
+        rest = rest - term.astype(F32)
+        for q in range(PARTS):
+            r = iota((128, WIDE), 0)
+            matrix = (r == 4 * q + iota((128, WIDE), 1) // HEAD_DIM).astype(F32).astype(BF16)
+            wide[q] = wide[q] + dot(term, matrix)
+    for q in range(PARTS):
+        decay_wide[2 * q] = wide[q][:, :128]
+        decay_wide[2 * q + 1] = wide[q][:, 128:]
+    own()
+    lax.fori_loop(0, PARTS, lambda p, c: (members(p), c)[1], 0)
     sq_ref[...] = jnp.zeros_like(sq_ref)
     lax.fori_loop(0, PARTS, lambda p, c: (finish(p), c)[1], 0)
 
-    sums = exact_dot(jnp.ones((8, 128), F32), sq_ref[...], ((1,), (1,)))
+    def over_columns(v):
+        return lax.dot_general(
+            jnp.ones((16, 128), BF16), v, (((1,), (1,)), ((), ())), preferred_element_type=F32
+        )
+
+    high = sq_ref[...].astype(BF16)
+    low = (sq_ref[...] - high.astype(F32)).astype(BF16)
+    sums = over_columns(high) + over_columns(low)
     n_send[0] = sums[0:1]
     n_recv[tp] = sums[0:1]
 
@@ -570,34 +686,22 @@
         to_tp(i).start()
     for i in range(1, tp_size):
         to_tp(i).wait_recv()
-    n_rows[...] = jnp.zeros_like(n_rows)
-    for k in range(tp_size):
-        n_rows[k : k + 1, :] = n_recv[k]
-    everyone = exact_dot(n_rows[...], jnp.ones((8, 128), F32), ((0,), (0,)))
-    sq_ref[...] = lax.rsqrt(everyone * (1.0 / (PARTS * WIDE * tp_size)) + EPSILON)
-
-    def out_copy(p):
-        return pltpu.make_async_copy(
-            o_ref.at[p], out_hbm.at[:, pl.ds(p * WIDE, WIDE)], out_sem.at[p]
-        )
-
-    def write(p, carry):
-        gain = norm_ref[p]
-        for c in range(subs):
-            at = slice(c * SUB, (c + 1) * SUB)
-            scale = sq_ref[at, :]
-            scale = jnp.concatenate([scale, scale], axis=1)
-            o_ref[p, at, :] = (y_ref[p, at, :] * scale * gain).astype(BF16)
-        return carry
-
-    for p in range(PARTS):
-        write(p, 0)
-        out_copy(p).start()
+    everyone = n_recv[0]
+    for k in range(1, tp_size):
+        everyone = everyone + n_recv[k]
+    scale = lax.rsqrt(everyone * (1.0 / (PARTS * WIDE * tp_size)) + EPSILON)
+    high = scale.astype(BF16).astype(F32)
+    row = iota((16, tokens), 0)
+    terms = jnp.where(row == 0, high, jnp.where(row == 1, scale - high, 0.0)).astype(BF16)
+    sq_ref[...] = lax.dot_general(
+        terms, jnp.ones((16, 128), BF16), (((0,), (0,)), ((), ())), preferred_element_type=F32
+    )
 
     for halo in halos:
         halo.wait_send()
     for i in range(1, 4):
         near_decay(i).wait_send()
+        edge_to(i).wait_send()
     lax.fori_loop(1, QUADS, lambda i, c: (far_decay(i).wait_send(), c)[1], 0)
     for p in range(PARTS):
         for i in range(1, 4):
@@ -612,8 +716,22 @@
     lax.fori_loop(1, QUADS, lambda i, c: (from_owner(i).wait_send(), c)[1], 0)
     for i in range(1, tp_size):
         to_tp(i).wait_send()
-    for p in range(PARTS):
-        out_copy(p).wait()
+
+
+def write(y_ref, scale_ref, norm_ref, out_hbm, out_ref, sem):
+    def copy(i):
+        return pltpu.make_async_copy(out_ref.at[i], out_hbm.at[pl.ds(i * 128, 128)], sem.at[i])
+
+    blocks = out_ref.shape[0]
+    for i in range(blocks):
+        at = slice(i * 128, (i + 1) * 128)
+        scale = scale_ref[at, :]
+        scale = jnp.concatenate([scale, scale], axis=1)
+        for p in range(PARTS):
+            out_ref[i, :, p * WIDE : (p + 1) * WIDE] = (y_ref[p, at, :] * scale * norm_ref[p]).astype(BF16)
+        copy(i).start()
+    for i in range(blocks):
+        copy(i).wait()
 
 
 def body(x_in, bc_in, z_gate, decay_rate, step_size, d_skip, conv_x, conv_bc, norm_weight, lengths):
@@ -625,22 +743,31 @@
     hbm = pl.BlockSpec(memory_space=pl.ANY)
     dma = pltpu.SemaphoreType.DMA
     split_taps = conv_x.reshape(4, PARTS, WIDE).transpose(1, 0, 2)
-    return pl.pallas_call(
+    gated, scale = pl.pallas_call(
         functools.partial(kernel, tp_size),
-        out_shape=jax.ShapeDtypeStruct((tokens, columns), BF16),
-        in_specs=[pl.BlockSpec(memory_space=pltpu.SMEM), hbm, vmem, hbm] + [vmem] * 6,
-        out_specs=hbm,
+        out_shape=[pltpu.VMEM((PARTS, tokens, WIDE), F32), pltpu.VMEM((tokens, 128), F32)],
+        in_specs=[pl.BlockSpec(memory_space=pltpu.SMEM), hbm, vmem, hbm] + [vmem] * 5,
+        out_specs=[vmem, vmem],
         scratch_shapes=[
             pltpu.VMEM((PARTS, 16 + tokens, WIDE), BF16),
             pltpu.VMEM((PARTS, tokens, WIDE), BF16),
+            pltpu.VMEM((PARTS, 32, WIDE), BF16),
+            pltpu.VMEM((32, 2 * STATE), BF16),
+            pltpu.VMEM((SUB, 2 * STATE), BF16),
             pltpu.VMEM((16 + tokens, 2 * STATE), BF16),
-            pltpu.VMEM((subs, 3 * SUB, 80), BF16),
+            pltpu.VMEM((-(-subs // 3), 576, 208), BF16),
+            pltpu.VMEM((-(-subs // 4), 4 * STATE, 4 * SUB), BF16),
             pltpu.VMEM((subs, SUB, STATE + SUB), BF16),
             pltpu.VMEM((PARTS, subs, STATE + SUB, WIDE), BF16),
-            pltpu.VMEM((subs, STATE, SUB), BF16),
             pltpu.VMEM((tokens, STATE), BF16),
             pltpu.VMEM((PARTS, tokens, WIDE), BF16),
             pltpu.VMEM((tokens, 32), F32),
+            pltpu.VMEM((tokens, 32), F32),
+            pltpu.VMEM((PARTS, subs, STATE, WIDE), F32),
+            pltpu.VMEM((3, 1, PARTS * WIDE + STATE), F32),
+            pltpu.VMEM((12, 1, PARTS * WIDE + STATE), F32),
+            pltpu.VMEM((4, 8, PARTS * WIDE + STATE), F32),
+            pltpu.VMEM((PARTS, 4, 32, WIDE), F32),
             pltpu.VMEM((16, 32), F32),
             pltpu.VMEM((16, 32), F32),
             pltpu.VMEM((tokens, 32), BF16),
@@ -648,12 +775,10 @@
             pltpu.VMEM((tokens, 32), BF16),
             pltpu.VMEM((64, 32), BF16),
             pltpu.VMEM((PARTS, tokens, WIDE), F32),
-            pltpu.VMEM((PARTS, tokens, WIDE), F32),
-            pltpu.VMEM((tokens, 128), F32),
-            pltpu.VMEM((PARTS, tokens, WIDE), BF16),
             pltpu.VMEM((4 * QUADS, 1, 128), F32),
             pltpu.VMEM((4 * QUADS, 128), F32),
             pltpu.VMEM((8, 4 * QUADS, 128), F32),
+            pltpu.VMEM((PARTS, 8, WIDE), F32),
             pltpu.VMEM((PARTS, 4, 32, WIDE), BF16),
             pltpu.VMEM((PARTS, 4, 32, WIDE), BF16),
             pltpu.VMEM((PARTS, 4, 16, 128), BF16),
@@ -664,11 +789,11 @@
             pltpu.VMEM((PARTS, 4, 32, WIDE), BF16),
             pltpu.VMEM((1, 1, tokens), F32),
             pltpu.VMEM((tp_size, 1, tokens), F32),
-            pltpu.VMEM((8, tokens), F32),
             dma((2 * PARTS,)),
-            dma((PARTS,)),
             dma((PARTS + 1,)),
             dma((PARTS + 1,)),
+            dma((4,)),
+            dma((4,)),
             dma((4,)),
             dma((4,)),
             dma((QUADS,)),
@@ -692,13 +817,20 @@
         x_in,
         bc_in,
         z_gate,
-        decay_rate,
-        step_size,
+        decay_rate.T,
+        step_size.T,
         d_skip.reshape(1, heads),
         split_taps,
         conv_bc,
-        norm_weight.reshape(PARTS, 1, WIDE),
     )
+    return pl.pallas_call(
+        write,
+        out_shape=jax.ShapeDtypeStruct((tokens, columns), BF16),
+        in_specs=[vmem] * 3,
+        out_specs=hbm,
+        scratch_shapes=[pltpu.VMEM((tokens // 128, 128, columns), BF16), dma((tokens // 128,))],
+        compiler_params=pltpu.CompilerParams(vmem_limit_bytes=8 * 1024 * 1024),
+    )(gated, scale, norm_weight.reshape(PARTS, 1, WIDE))
 
 
 def solution(mesh):

time: 85.6 us -> 61.2 us (0.71)
  Pallas kernels: 79.2 us -> 61 us
  local copies, waits for them, and re-layouts: 6.09 us -> 0.01 us
    pallas_call x1 -> x2, Pallas kernels: 79.2 us -> 61 us  [the longest x1 59.7 us: body(): pl.pallas_call(functools.partial(kernel, tp_size), out_shape=[pltpu.VMEM(...]
    unnamed x3 -> x2, local copies, waits for them, and re-layouts: 6.09 us -> 0.01 us
where the time goes in v2:
time: 61.2 us; the launch traced here: 61 us
  Pallas kernels  61 us (100%)
    pallas_call x1, Pallas kernels, body(): pl.pallas_call(functools.partial(kernel, tp_size), out_shape=[pltpu.VMEM(...  59.7 us
    pallas_call x1, Pallas kernels, body(): pl.pallas_call(write, out_shape=jax.ShapeDtypeStruct((tokens, columns), B...  1.23 us

profile of v2, /device:TPU:1, one launch (start us, length us, event | category | flops | bytes accessed | tf_op | source)
XLA Modules:
  0.0 61.0 jit_solution(17983040914037061340)
XLA Ops:
  0.0 0.0 copy-start
  0.0 59.7 %shard_map.100 = (f32[4,768,256]{2,1,0:T(8,128)S(1)}, f32[768,128]{1,0:T(8,128)S(1)}) custom-call(s32[4]{0:T(128)} %len_ref.1, bf16[768,1024]{1,0:T(8,128)(2,1)} %x_hbm.1, bf16[768,256]{1,0:T(8,128)(2,1)} %bc_ref.1, bf16[768,1024]{1,0:T(8,128)(2,1)} %z_hbm.1, f32[16,768]{1,0:T(8,128)} %bitcast.8, f32[16,768]{1,0:T(8,128)} %bitcast.9, f32[1,16]{1,0:T(1,128)} %bitcast.11, ...), custom_call_target="tpu_custom_call" | custom-call | tf_op jit(solution)/shard_map/pallas_call | solution.py:746
  59.8 0.0 copy-done
  59.8 1.2 %shard_map.101 = bf16[768,1024]{1,0:T(8,128)(2,1)} custom-call(f32[4,768,256]{2,1,0:T(8,128)S(1)} %get-tuple-element.7.y_ref, f32[768,128]{1,0:T(8,128)S(1)} %get-tuple-element.8.scale_ref, f32[4,1,256]{2,1,0:T(1,128)S(1)} %bitcast.7), custom_call_target="tpu_custom_call" | custom-call | tf_op jit(solution)/shard_map/pallas_call | solution.py:826
Async XLA Ops:
  0.0 59.8 %copy-start = (f32[1024]{0:T(1024)S(1)}, f32[1024]{0:T(1024)}, u32[]{:S(2)}) copy-start(f32[1024]{0:T(1024)} %param.18) | copy-start | bytes 12292

commit v3 on v2

--- a/solution.py
+++ b/solution.py
@@ -45,22 +45,27 @@
 
 def kernel(
     tp_size,
+    len_hbm,
+    x_hbm,
+    bc_hbm,
+    z_hbm,
+    rate_hbm,
+    step_hbm,
+    skip_hbm,
+    conv_x_hbm,
+    conv_bc_hbm,
+    y_ref,
+    sq_ref,
     len_ref,
-    x_hbm,
-    bc_ref,
-    z_hbm,
     rate_ref,
     step_ref,
     skip_ref,
     conv_x_ref,
     conv_bc_ref,
-    y_ref,
-    sq_ref,
     xs,
     zs,
     x_edge,
     bc_edge,
-    bc0_ref,
     bcs,
     shift_ref,
     group_ref,
@@ -80,6 +85,9 @@
     f_ref,
     e_ref,
     ef_ref,
+    g_all,
+    keys_all,
+    keys_t,
     rows_ref,
     g_ref,
     decay_all,
@@ -129,8 +137,16 @@
     def quad_peer(i):
         return quad * 4 + (member + i) % 4
 
-    def far_peer(i):
-        return ((quad + i) % QUADS) * 4 + member
+    owners = [(p, r) for p in range(PARTS) for r in range(2)]
+    is_owner = quad % 2 == 1
+    my_part = quad // 4
+    my_half = (quad % 4) // 2
+
+    def owner_quad(p, r):
+        return 4 * p + 1 + 2 * r
+
+    def same_place(q):
+        return 4 * q + member
 
     def x_copy(p):
         return pltpu.make_async_copy(
@@ -144,10 +160,39 @@
 
     barrier = pltpu.get_barrier_semaphore()
 
+    small = [
+        pltpu.make_async_copy(source, target, in_sem.at[2 * PARTS + k])
+        for k, (source, target) in enumerate(
+            [
+                (rate_hbm, rate_ref),
+                (step_hbm, step_ref),
+                (len_hbm, len_ref),
+                (skip_hbm, skip_ref),
+                (bc_hbm, bcs.at[pl.ds(16, tokens)]),
+                (conv_bc_hbm, conv_bc_ref),
+                (conv_x_hbm, conv_x_ref),
+            ]
+        )
+    ]
+    for copy in small:
+        copy.start()
+    for p in range(PARTS):
+        x_copy(p).start()
+
     def greet(peer):
         pl.semaphore_signal(barrier, inc=1, device_id={"slot": peer}, device_id_type=MESH)
 
-    lax.fori_loop(1, QUADS, lambda i, c: (greet(far_peer(i)), c)[1], 0)
+    for p, r in owners:
+
+        @pl.when(quad != owner_quad(p, r))
+        def _():
+            greet(same_place(owner_quad(p, r)))
+
+    @pl.when(is_owner)
+    def _():
+        for q in range(0, QUADS, 2):
+            greet(same_place(q))
+
     for i in range(1, 4):
         greet(quad_peer(i))
     greet(after)
@@ -156,10 +201,8 @@
         pl.semaphore_signal(
             barrier, inc=1, device_id={"tp": (tp + i) % tp_size}, device_id_type=MESH
         )
-    for p in range(PARTS):
-        x_copy(p).start()
-    for p in range(PARTS):
-        z_copy(p).start()
+    for copy in small[:4]:
+        copy.wait()
 
     ends = []
     total = 0
@@ -200,6 +243,15 @@
         open_rows = start_of(pos, ends[:3]) < first_row
         ef_ref[at, :] = two_terms(jnp.where(open_rows, jnp.exp(-(offset + cum)), 0.0))
         offset = offset + end
+    left_over = jnp.zeros((1, 32), F32)
+    last_start = start_of(jnp.zeros((SUB, 32), jnp.int32) + (first_row + tokens - 1), ends)
+    for c in reversed(range(subs)):
+        at = slice(c * SUB, (c + 1) * SUB)
+        end = end_ref[c : c + 1, :]
+        pos = first_row + c * SUB + iota((SUB, 32), 0)
+        fade = jnp.exp(-(left_over + (end - cum_ref[at, :]))) * st_ref[at, :]
+        g_all[at, :] = two_terms(jnp.where(pos >= last_start, fade, 0.0))
+        left_over = left_over + end
     last_pos = first_row + tokens - 1 + jnp.zeros((1, 32), jnp.int32)
     whole = start_of(last_pos, ends[:3]) < first_row
     decay = jnp.where(whole, jnp.exp(-offset), 0.0)
@@ -230,7 +282,9 @@
             shift_ref[k, d * count : (d + 1) * count, : count + 16] = one
 
     bcs[:16, :] = jnp.zeros((16, 2 * STATE), BF16)
-    bcs[16:, :] = bc_ref[...]
+    small[4].wait()
+    small[5].wait()
+    small[6].wait()
     for p in range(PARTS):
         xs[p, :16, :] = jnp.zeros((16, WIDE), BF16)
 
@@ -248,12 +302,10 @@
 
     groups = [(c, min(4, subs - c)) for c in range(0, subs, 4)]
 
-    def keys_and_queries(c, bc, again=False):
+    def keys_and_queries(c):
         base = first_row + c * SUB
-        key, query = bc[:, :STATE], bc[:, STATE:]
-        c_ref[c * SUB : (c + 1) * SUB, :] = query
-        if c == 0:
-            bc0_ref[...] = bc
+        at = slice(c * SUB, (c + 1) * SUB)
+        key, query = keys_all[at, :], c_ref[at, :]
         scores = lax.dot_general(query, key, (((1,), (1,)), ((), ())), preferred_element_type=F32)
         t = iota((SUB, SUB), 0)
         s = iota((SUB, SUB), 1)
@@ -264,15 +316,16 @@
         left_ref[c, :, :STATE] = jnp.where(from_before, query.astype(F32), 0.0).astype(BF16)
         last = start_of(jnp.zeros((SUB, STATE), jnp.int32) + (base + SUB - 1), ends)
         keys = jnp.where(row >= last, key.astype(F32), 0.0)
-        if not again:
-            g, i = c // 4, c % 4
-            group_ref[g, i * STATE : (i + 1) * STATE, i * SUB : (i + 1) * SUB] = keys.T.astype(BF16)
-
-    group_ref[...] = jnp.zeros_like(group_ref)
+        g, i = c // 4, c % 4
+        group_ref[g, i * STATE : (i + 1) * STATE, i * SUB : (i + 1) * SUB] = keys.T.astype(BF16)
+
     for k, (row, count) in enumerate(blocks):
         bc = conv(bcs[row : row + count + 16, :], block_shifts(k), conv_bc_ref[...])
-        for i in range(count // SUB):
-            keys_and_queries(row // SUB + i, bc[i * SUB : (i + 1) * SUB])
+        keys_all[row : row + count, :] = bc[:, :STATE]
+        c_ref[row : row + count, :] = bc[:, STATE:]
+    for b in range(tokens // width):
+        at = slice(b * width, (b + 1) * width)
+        keys_t[:, at] = keys_all[at, :].astype(F32).T.astype(BF16)
 
     def widen_matrix(p, rows):
         r = iota((rows, WIDE), 0) % 16
@@ -281,78 +334,56 @@
     def row_factors(p):
         return dot(rows_ref[...], widen_matrix(p, 32))
 
-    def later_subs(p, carry):
-        x_copy(p).wait()
+    def later_subs(p):
         taps = conv_x_ref[p]
-        wide_f = dot(f_ref[...], widen_matrix(p, 32))
-        rows = row_factors(p)
+        wide_g = dot(g_all[...], widen_matrix(p, 32))
         parts = []
         for k, (row, count) in enumerate(blocks):
             values = conv(xs[p, row : row + count + 16, :], block_shifts(k), taps)
             xconv[p, row : row + count, :] = values
-            scaled = values.astype(F32) * wide_f[row : row + count]
+            scaled = values.astype(F32) * wide_g[row : row + count]
             if row == 0:
                 scaled = jnp.where(iota(scaled.shape, 0) >= 3, scaled, 0.0)
-            scaled = scaled.astype(BF16)
-            for i in range(count // SUB):
-                one = scaled[i * SUB : (i + 1) * SUB]
-                right_ref[p, row // SUB + i, STATE:, :] = one
-                parts.append(one)
-        state = jnp.zeros((STATE, WIDE), F32)
+            parts.append(scaled.astype(BF16))
+        state = dot(keys_t[...], jnp.concatenate(parts, axis=0))
+        l_send[p] = state.astype(BF16).reshape(4, 32, WIDE)
+        q_recv[p, member] = l_send[p, member]
+
+    def add_subs(p):
+        wide_f = dot(f_ref[...], widen_matrix(p, 32))
         for g, (first, many) in enumerate(groups):
-            scaled = jnp.concatenate(parts[first : first + many], axis=0)
+            at = slice(first * SUB, (first + many) * SUB)
+            scaled = (xconv[p, at, :].astype(F32) * wide_f[at]).astype(BF16)
             adds = dot(group_ref[g, : many * STATE, : many * SUB], scaled)
             for i in range(many):
-                c = first + i
-                add = adds[i * STATE : (i + 1) * STATE]
-                u_ref[p, c] = add
-                if c == 0:
-                    state = rows[16:17] * add
-                else:
-                    state = rows[32 + c : 33 + c] * rows[c : c + 1] * state + rows[16 + c : 17 + c] * add
-        l_send[p] = state.astype(BF16).reshape(4, 32, WIDE)
-        q_recv[p, member] = l_send[p, member]
-        return carry
-
-    def edge_fade(rows):
-        fade = rows[16:17]
-        for c in range(1, subs):
-            fade = fade * rows[32 + c : 33 + c] * rows[c : c + 1]
-        return fade
-
-    edge_shape = (16, STATE)
+                right_ref[p, first + i, STATE:, :] = scaled[i * SUB : (i + 1) * SUB]
+                u_ref[p, first + i] = adds[i * STATE : (i + 1) * STATE]
 
     def edge():
         shifts = jnp.concatenate(shifts_at(0, 16), axis=0)
         halos[PARTS].wait_recv()
         bc = conv(bc_edge[...], shifts, conv_bc_ref[...])
-        bc0_ref[0:16, :] = bc
-        row = first_row + iota(edge_shape, 0)
-        last = start_of(jnp.zeros(edge_shape, jnp.int32) + (first_row + SUB - 1), ends)
-        keys = jnp.where(row >= last, bc[:, :STATE].astype(F32), 0.0)
+        keys_all[0:16, :] = bc[:, :STATE]
+        c_ref[0:16, :] = bc[:, STATE:]
+        keys = bc[:, :STATE].astype(F32)
         for t in range(3):
             e_send[t, :, PARTS * WIDE :] = keys[t : t + 1]
         for p in range(PARTS):
             halos[p].wait_recv()
         every = range(PARTS)
-        rows = [row_factors(p) for p in every]
-        wide_f = [dot(f_ref[0:16, :], widen_matrix(p, 32)) for p in every]
+        wide_g = [dot(g_all[0:16, :], widen_matrix(p, 32)) for p in every]
         values = [conv(x_edge[p], shifts, conv_x_ref[p]) for p in every]
-        scaled = [(values[p].astype(F32) * wide_f[p]).astype(BF16) for p in every]
         for p in every:
-            faded = scaled[p].astype(F32) * edge_fade(rows[p])
+            faded = values[p].astype(F32) * wide_g[p]
             for t in range(3):
                 e_send[t, :, p * WIDE : (p + 1) * WIDE] = faded[t : t + 1]
         for i in range(1, 4):
             edge_to(i).start()
-        first_three = jnp.where(iota(edge_shape, 0) < 3, keys, 0.0).astype(BF16)
         for p in every:
             xconv[p, 0:16, :] = values[p]
-            right_ref[p, 0, STATE : STATE + 16, :] = scaled[p]
-            u_ref[p, 0] += lax.dot_general(
-                first_three, scaled[p], (((0,), (0,)), ((), ())), preferred_element_type=F32
-            )
-        keys_and_queries(0, bc0_ref[...], again=True)
+        group_ref[...] = jnp.zeros_like(group_ref)
+        for c in range(subs):
+            keys_and_queries(c)
 
     def edge_to(i):
         return pltpu.make_async_remote_copy(
@@ -391,10 +422,15 @@
             if c + 1 < subs:
                 state = rows[32 + c : 33 + c] * faded + rows[16 + c : 17 + c] * u_ref[p, c]
 
-    lax.fori_loop(0, PARTS, later_subs, 0)
+    for p in range(PARTS):
+        x_copy(p).wait()
+    for p in range(PARTS):
+        later_subs(p)
     for p in range(PARTS):
         x_edge[p, 16:, :] = xs[p, 16:32, :]
-    bc_edge[16:, :] = bc_ref[:16, :]
+    bc_edge[16:, :] = bcs[16:32, :]
+    for p in range(PARTS):
+        z_copy(p).start()
 
     def to_quad(p, i):
         return pltpu.make_async_remote_copy(
@@ -406,7 +442,7 @@
             device_id_type=MESH,
         )
 
-    pl.semaphore_wait(barrier, 2 + 3 + (QUADS - 1) + (tp_size - 1))
+    pl.semaphore_wait(barrier, 2 + 3 + (tp_size - 1) + jnp.where(is_owner, QUADS - 1, len(owners)))
     halos = []
     for p in range(PARTS):
         halos.append(
@@ -421,7 +457,7 @@
         )
     halos.append(
         pltpu.make_async_remote_copy(
-            bc_ref.at[pl.ds(tokens - 16, 16)],
+            bc_hbm.at[pl.ds(tokens - 16, 16)],
             bc_edge.at[pl.ds(0, 16)],
             halo_send.at[PARTS],
             halo_recv.at[PARTS],
@@ -443,15 +479,22 @@
             device_id_type=MESH,
         )
 
-    def far_decay(i):
+    def far_decay(p, r):
         return pltpu.make_async_remote_copy(
             decay_all.at[pl.ds(quad * 4, 4)],
             decay_all.at[pl.ds(quad * 4, 4)],
-            d_send2.at[i],
-            d_recv2.at[i],
-            device_id={"slot": far_peer(i)},
-            device_id_type=MESH,
-        )
+            d_send2.at[2 * p + r],
+            d_recv2.at[quad],
+            device_id={"slot": same_place(owner_quad(p, r))},
+            device_id_type=MESH,
+        )
+
+    def each_far_owner(act):
+        for p, r in owners:
+
+            @pl.when(quad != owner_quad(p, r))
+            def _():
+                act(p, r)
 
     for p in range(PARTS):
         for i in range(1, 4):
@@ -460,29 +503,23 @@
         near_decay(i).start()
 
 
-    def owner_of(p, tile):
-        return 4 * tile + (p + 4 - tile) % 4
-
-    def to_owner(p, tile):
+    def to_owner(p, r):
         return pltpu.make_async_remote_copy(
-            t_send.at[p, tile],
+            t_send.at[p, r],
             o_recv.at[quad],
-            s2.at[p, tile],
+            s2.at[p, r],
             r2.at[quad],
-            device_id={"slot": owner_of(p, tile) * 4 + member},
-            device_id_type=MESH,
-        )
-
-    my_part = (quad // 4 + quad % 4) % 4
-    my_tile = quad // 4
-
-    def from_owner(i):
+            device_id={"slot": same_place(owner_quad(p, r))},
+            device_id_type=MESH,
+        )
+
+    def from_owner(q):
         return pltpu.make_async_remote_copy(
-            o_send.at[(quad + i) % QUADS],
-            g_recv.at[my_part, my_tile],
-            s3.at[i],
-            r3.at[my_part, my_tile],
-            device_id={"slot": far_peer(i)},
+            o_send.at[q],
+            g_recv.at[my_part, my_half],
+            s3.at[q],
+            r3.at[my_part, my_half],
+            device_id={"slot": same_place(q)},
             device_id_type=MESH,
         )
 
@@ -509,67 +546,60 @@
             n_state[p, i] = new
             run = decay_of(p, i) * run + new
         run = run.astype(BF16)
-        for tile in range(4):
-            r, l = tile // 2, tile % 2
-            t_send[p, tile] = run[16 * r : 16 * r + 16, 128 * l : 128 * l + 128]
-        for tile in range(4):
-            mine = owner_of(p, tile) == quad
+        for r in range(2):
+            t_send[p, r] = run[16 * r : 16 * r + 16]
+            mine = owner_quad(p, r) == quad
 
             @pl.when(mine)
             def _():
-                o_recv[quad] = t_send[p, tile]
+                o_recv[quad] = t_send[p, r]
 
             @pl.when(jnp.logical_not(mine))
             def _():
-                to_owner(p, tile).start()
+                to_owner(p, r).start()
 
     def own():
-        def wait_one(i, c):
-            source = (quad + i) % QUADS
-            pltpu.make_async_remote_copy(
-                t_send.at[0, 0],
-                o_recv.at[source],
-                s2.at[0, 0],
-                r2.at[source],
-                device_id={"slot": far_peer(i)},
-                device_id_type=MESH,
-            ).wait_recv()
-            return c
-
-        lax.fori_loop(1, QUADS, wait_one, 0)
-        tile = 2 * my_part + my_tile % 2
-        run = jnp.zeros((16, 128), F32)
+        run = jnp.zeros((16, WIDE), F32)
         for q in range(QUADS):
             o_send[q] = run.astype(BF16)
-            fade = decay_wide[tile, 4 * q : 4 * q + 1, :]
+            other = quad != q
+
+            @pl.when(other)
+            def _():
+                from_owner(q).start()
+                to_owner_of(q).wait_recv()
+
+            fade = decay_wide[4 * q : 4 * q + 1, :]
             for i in range(1, 4):
-                fade = fade * decay_wide[tile, 4 * q + i : 4 * q + i + 1, :]
+                fade = fade * decay_wide[4 * q + i : 4 * q + i + 1, :]
             run = fade * run + o_recv[q].astype(F32)
-        g_recv[my_part, my_tile] = o_send[quad]
-        lax.fori_loop(1, QUADS, lambda i, c: (from_owner(i).start(), c)[1], 0)
+        g_recv[my_part, my_half] = o_send[quad]
+
+    def to_owner_of(q):
+        return pltpu.make_async_remote_copy(
+            t_send.at[0, 0],
+            o_recv.at[q],
+            s2.at[0, 0],
+            r2.at[q],
+            device_id={"slot": same_place(q)},
+            device_id_type=MESH,
+        )
 
     def members(p):
-        for tile in range(4):
-
-            @pl.when(owner_of(p, tile) != quad)
+        for r in range(2):
+
+            @pl.when(owner_quad(p, r) != quad)
             def _():
                 pltpu.make_async_remote_copy(
                     o_send.at[0],
-                    g_recv.at[p, tile],
+                    g_recv.at[p, r],
                     s3.at[0],
-                    r3.at[p, tile],
+                    r3.at[p, r],
                     device_id={"slot": after},
                     device_id_type=MESH,
                 ).wait_recv()
 
-        tiles = [g_recv[p, tile].astype(F32) for tile in range(4)]
-        run = jnp.concatenate(
-            [
-                jnp.concatenate([tiles[0], tiles[1]], axis=1),
-                jnp.concatenate([tiles[2], tiles[3]], axis=1),
-            ],
-            axis=0,
-        )
+        run = g_recv[p].reshape(32, WIDE).astype(F32)
         for i in range(4):
             p_send[p, i] = run.astype(BF16)
             if i < 3:
@@ -602,6 +632,7 @@
             sq_ref[at, :] += square[:, :128] + square[:, 128:]
 
     def second_pass(p, carry):
+        add_subs(p)
         chain(p)
         local(p)
         return carry
@@ -610,7 +641,7 @@
     lax.fori_loop(0, 2, second_pass, 0)
     for i in range(1, 4):
         near_decay(i).wait_recv()
-    lax.fori_loop(1, QUADS, lambda i, c: (far_decay(i).start(), c)[1], 0)
+    each_far_owner(lambda p, r: far_decay(p, r).start())
     near = jnp.zeros((8, 128), F32)
     for i in range(4):
         near = jnp.where(iota((8, 128), 0) == i, decay_all[quad * 4 + i], near)
@@ -629,35 +660,50 @@
         quad_totals(p)
     lax.fori_loop(2, PARTS, second_pass, 0)
 
-    def wait_decay(i, c):
-        source = ((quad + QUADS - i) % QUADS) * 4
-        pltpu.make_async_remote_copy(
-            decay_all.at[pl.ds(source, 4)],
-            decay_all.at[pl.ds(source, 4)],
-            d_send2.at[i],
-            d_recv2.at[i],
-            device_id={"slot": far_peer(i)},
-            device_id_type=MESH,
-        ).wait_recv()
-        return c
-
-    lax.fori_loop(1, QUADS, wait_decay, 0)
-    for k in range(slots):
-        decay_rows[k : k + 1, :] = decay_all[k]
-    rest = decay_rows[...]
-    wide = [jnp.zeros((slots, WIDE), F32) for _ in range(PARTS)]
-    for _ in range(3):
-        term = rest.astype(BF16)
-        rest = rest - term.astype(F32)
-        for q in range(PARTS):
-            r = iota((128, WIDE), 0)
-            matrix = (r == 4 * q + iota((128, WIDE), 1) // HEAD_DIM).astype(F32).astype(BF16)
-            wide[q] = wide[q] + dot(term, matrix)
-    for q in range(PARTS):
-        decay_wide[2 * q] = wide[q][:, :128]
-        decay_wide[2 * q + 1] = wide[q][:, 128:]
-    own()
+    for halo in halos:
+        halo.wait_send()
+    for i in range(1, 4):
+        near_decay(i).wait_send()
+        edge_to(i).wait_send()
+        for p in range(PARTS):
+            to_quad(p, i).wait_send()
+    each_far_owner(lambda p, r: far_decay(p, r).wait_send())
+
+    @pl.when(is_owner)
+    def _():
+        for q in range(QUADS):
+
+            @pl.when(quad != q)
+            def _():
+                pltpu.make_async_remote_copy(
+                    decay_all.at[pl.ds(4 * q, 4)],
+                    decay_all.at[pl.ds(4 * q, 4)],
+                    d_send2.at[0],
+                    d_recv2.at[q],
+                    device_id={"slot": same_place(q)},
+                    device_id_type=MESH,
+                ).wait_recv()
+
+        for k in range(slots):
+            decay_rows[k : k + 1, :] = decay_all[k]
+        rest = decay_rows[...]
+        wide = jnp.zeros((slots, WIDE), F32)
+        r = iota((128, WIDE), 0)
+        matrix = (r == 4 * my_part + iota((128, WIDE), 1) // HEAD_DIM).astype(F32).astype(BF16)
+        for _ in range(3):
+            term = rest.astype(BF16)
+            rest = rest - term.astype(F32)
+            wide = wide + dot(term, matrix)
+        decay_wide[...] = wide
+        own()
+
+    each_far_owner(lambda p, r: to_owner(p, r).wait_send())
     lax.fori_loop(0, PARTS, lambda p, c: (members(p), c)[1], 0)
+
+    @pl.when(is_owner)
+    def _():
+        lax.fori_loop(1, QUADS, lambda i, c: (from_owner((quad + i) % QUADS).wait_send(), c)[1], 0)
+
     sq_ref[...] = jnp.zeros_like(sq_ref)
     lax.fori_loop(0, PARTS, lambda p, c: (finish(p), c)[1], 0)
 
@@ -684,6 +730,9 @@
 
     for i in range(1, tp_size):
         to_tp(i).start()
+    for p in range(PARTS):
+        for i in range(1, 4):
+            to_member(p, i).wait_send()
     for i in range(1, tp_size):
         to_tp(i).wait_recv()
     everyone = n_recv[0]
@@ -697,23 +746,6 @@
         terms, jnp.ones((16, 128), BF16), (((0,), (0,)), ((), ())), preferred_element_type=F32
     )
 
-    for halo in halos:
-        halo.wait_send()
-    for i in range(1, 4):
-        near_decay(i).wait_send()
-        edge_to(i).wait_send()
-    lax.fori_loop(1, QUADS, lambda i, c: (far_decay(i).wait_send(), c)[1], 0)
-    for p in range(PARTS):
-        for i in range(1, 4):
-            to_quad(p, i).wait_send()
-            to_member(p, i).wait_send()
-        for tile in range(4):
-
-            @pl.when(owner_of(p, tile) != quad)
-            def _():
-                to_owner(p, tile).wait_send()
-
-    lax.fori_loop(1, QUADS, lambda i, c: (from_owner(i).wait_send(), c)[1], 0)
     for i in range(1, tp_size):
         to_tp(i).wait_send()
 
@@ -746,14 +778,19 @@
     gated, scale = pl.pallas_call(
         functools.partial(kernel, tp_size),
         out_shape=[pltpu.VMEM((PARTS, tokens, WIDE), F32), pltpu.VMEM((tokens, 128), F32)],
-        in_specs=[pl.BlockSpec(memory_space=pltpu.SMEM), hbm, vmem, hbm] + [vmem] * 5,
+        in_specs=[hbm] * 9,
         out_specs=[vmem, vmem],
         scratch_shapes=[
+            pltpu.SMEM((4,), jnp.int32),
+            pltpu.VMEM((heads, tokens), F32),
+            pltpu.VMEM((heads, tokens), F32),
+            pltpu.VMEM((1, heads), F32),
+            pltpu.VMEM((PARTS, 4, WIDE), F32),
+            pltpu.VMEM((4, 2 * STATE), F32),
             pltpu.VMEM((PARTS, 16 + tokens, WIDE), BF16),
             pltpu.VMEM((PARTS, tokens, WIDE), BF16),
             pltpu.VMEM((PARTS, 32, WIDE), BF16),
             pltpu.VMEM((32, 2 * STATE), BF16),
-            pltpu.VMEM((SUB, 2 * STATE), BF16),
             pltpu.VMEM((16 + tokens, 2 * STATE), BF16),
             pltpu.VMEM((-(-subs // 3), 576, 208), BF16),
             pltpu.VMEM((-(-subs // 4), 4 * STATE, 4 * SUB), BF16),
@@ -773,23 +810,26 @@
             pltpu.VMEM((tokens, 32), BF16),
             pltpu.VMEM((tokens, 32), BF16),
             pltpu.VMEM((tokens, 32), BF16),
+            pltpu.VMEM((tokens, 32), BF16),
+            pltpu.VMEM((tokens, STATE), BF16),
+            pltpu.VMEM((STATE, tokens), BF16),
             pltpu.VMEM((64, 32), BF16),
             pltpu.VMEM((PARTS, tokens, WIDE), F32),
             pltpu.VMEM((4 * QUADS, 1, 128), F32),
             pltpu.VMEM((4 * QUADS, 128), F32),
-            pltpu.VMEM((8, 4 * QUADS, 128), F32),
+            pltpu.VMEM((4 * QUADS, WIDE), F32),
             pltpu.VMEM((PARTS, 8, WIDE), F32),
             pltpu.VMEM((PARTS, 4, 32, WIDE), BF16),
             pltpu.VMEM((PARTS, 4, 32, WIDE), BF16),
-            pltpu.VMEM((PARTS, 4, 16, 128), BF16),
-            pltpu.VMEM((QUADS, 16, 128), BF16),
-            pltpu.VMEM((QUADS, 16, 128), BF16),
-            pltpu.VMEM((PARTS, 4, 16, 128), BF16),
+            pltpu.VMEM((PARTS, 2, 16, WIDE), BF16),
+            pltpu.VMEM((QUADS, 16, WIDE), BF16),
+            pltpu.VMEM((QUADS, 16, WIDE), BF16),
+            pltpu.VMEM((PARTS, 2, 16, WIDE), BF16),
             pltpu.VMEM((PARTS, 4, 32, WIDE), BF16),
             pltpu.VMEM((PARTS, 4, 32, WIDE), BF16),
             pltpu.VMEM((1, 1, tokens), F32),
             pltpu.VMEM((tp_size, 1, tokens), F32),
-            dma((2 * PARTS,)),
+            dma((2 * PARTS + 7,)),
             dma((PARTS + 1,)),
             dma((PARTS + 1,)),
             dma((4,)),

time: 61.2 us -> 55.8 us (0.912)
  Pallas kernels: 61 us -> 55.6 us
    pallas_call x1, Pallas kernels: 59.7 us -> 54.4 us  [body(): pl.pallas_call(functools.partial(kernel, tp_size), out_shape=[pltpu.VMEM(...]
where the time goes in v3:
time: 55.8 us; the launch traced here: 55.6 us
  Pallas kernels  55.6 us (100%)
    pallas_call x1, Pallas kernels, body(): pl.pallas_call(functools.partial(kernel, tp_size), out_shape=[pltpu.VMEM(...  54.4 us
    pallas_call x1, Pallas kernels, body(): pl.pallas_call(write, out_shape=jax.ShapeDtypeStruct((tokens, columns), B...  1.23 us

profile of v3, /device:TPU:1, one launch (start us, length us, event | category | flops | bytes accessed | tf_op | source)
XLA Modules:
  0.0 55.6 jit_solution(1920993443981082016)
XLA Ops:
  0.0 0.0 copy-start
  0.0 54.4 %shard_map.100 = (f32[4,768,256]{2,1,0:T(8,128)S(1)}, f32[768,128]{1,0:T(8,128)S(1)}) custom-call(s32[4]{0:T(128)} %len_hbm.1, bf16[768,1024]{1,0:T(8,128)(2,1)} %x_hbm.1, bf16[768,256]{1,0:T(8,128)(2,1)} %bc_hbm.1, bf16[768,1024]{1,0:T(8,128)(2,1)} %z_hbm.1, f32[16,768]{1,0:T(8,128)} %bitcast.8, f32[16,768]{1,0:T(8,128)} %bitcast.9, f32[1,16]{1,0:T(1,128)} %bitcast.11, ...), custom_call_target="tpu_custom_call" | custom-call | tf_op jit(solution)/shard_map/pallas_call | solution.py:778
  54.4 0.0 copy-done
  54.4 1.2 %shard_map.101 = bf16[768,1024]{1,0:T(8,128)(2,1)} custom-call(f32[4,768,256]{2,1,0:T(8,128)S(1)} %get-tuple-element.7.y_ref, f32[768,128]{1,0:T(8,128)S(1)} %get-tuple-element.8.scale_ref, f32[4,1,256]{2,1,0:T(1,128)S(1)} %bitcast.7), custom_call_target="tpu_custom_call" | custom-call | tf_op jit(solution)/shard_map/pallas_call | solution.py:866
Async XLA Ops:
  0.0 54.4 %copy-start = (f32[1024]{0:T(1024)S(1)}, f32[1024]{0:T(1024)}, u32[]{:S(2)}) copy-start(f32[1024]{0:T(1024)} %param.18) | copy-start | bytes 12292

commit v4 on v3

--- a/solution.py
+++ b/solution.py
@@ -361,17 +361,16 @@
 
     def edge():
         shifts = jnp.concatenate(shifts_at(0, 16), axis=0)
-        halos[PARTS].wait_recv()
+        every = range(PARTS)
+        wide_g = [dot(g_all[0:16, :], widen_matrix(p, 32)) for p in every]
+        for halo in halos:
+            halo.wait_recv()
         bc = conv(bc_edge[...], shifts, conv_bc_ref[...])
         keys_all[0:16, :] = bc[:, :STATE]
         c_ref[0:16, :] = bc[:, STATE:]
         keys = bc[:, :STATE].astype(F32)
         for t in range(3):
             e_send[t, :, PARTS * WIDE :] = keys[t : t + 1]
-        for p in range(PARTS):
-            halos[p].wait_recv()
-        every = range(PARTS)
-        wide_g = [dot(g_all[0:16, :], widen_matrix(p, 32)) for p in every]
         values = [conv(x_edge[p], shifts, conv_x_ref[p]) for p in every]
         for p in every:
             faded = values[p].astype(F32) * wide_g[p]
@@ -379,6 +378,9 @@
                 e_send[t, :, p * WIDE : (p + 1) * WIDE] = faded[t : t + 1]
         for i in range(1, 4):
             edge_to(i).start()
+        for i in range(1, 4):
+            near_decay(i).wait_recv()
+        each_far_owner(lambda p, r: far_decay(p, r).start())
         for p in every:
             xconv[p, 0:16, :] = values[p]
         group_ref[...] = jnp.zeros_like(group_ref)
@@ -405,12 +407,16 @@
             for t in range(3):
                 e_rows[i, t : t + 1, :] = e_recv[i * 3 + t]
 
+        pick = (iota((32, STATE), 1) == member * 32 + iota((32, STATE), 0)).astype(F32).astype(BF16)
+        for i in range(4):
+            keys = e_rows[i, :, PARTS * WIDE :].astype(BF16)
+            keys = lax.dot_general(pick, keys, (((1,), (1,)), ((), ())), preferred_element_type=F32)
+            adds = dot(keys.astype(BF16), e_rows[i, :, : PARTS * WIDE].astype(BF16))
+            for p in range(PARTS):
+                n_state[p, i] = adds[:, p * WIDE : (p + 1) * WIDE]
+
     def quad_state(p, i):
-        pick = (iota((32, STATE), 1) == member * 32 + iota((32, STATE), 0)).astype(F32).astype(BF16)
-        keys = e_rows[i, :, PARTS * WIDE :].astype(BF16)
-        keys = lax.dot_general(pick, keys, (((1,), (1,)), ((), ())), preferred_element_type=F32)
-        values = e_rows[i, :, p * WIDE : (p + 1) * WIDE].astype(BF16)
-        return q_recv[p, i].astype(F32) + dot(keys.astype(BF16), values)
+        return q_recv[p, i].astype(F32) + n_state[p, i]
 
     def chain(p):
         rows = row_factors(p)
@@ -425,8 +431,6 @@
     for p in range(PARTS):
         x_copy(p).wait()
     for p in range(PARTS):
-        later_subs(p)
-    for p in range(PARTS):
         x_edge[p, 16:, :] = xs[p, 16:32, :]
     bc_edge[16:, :] = bcs[16:32, :]
     for p in range(PARTS):
@@ -496,11 +500,12 @@
             def _():
                 act(p, r)
 
-    for p in range(PARTS):
+    for i in range(1, 4):
+        near_decay(i).start()
+    for p in range(PARTS):
+        later_subs(p)
         for i in range(1, 4):
             to_quad(p, i).start()
-    for i in range(1, 4):
-        near_decay(i).start()
 
 
     def to_owner(p, r):
@@ -639,9 +644,6 @@
 
     edge()
     lax.fori_loop(0, 2, second_pass, 0)
-    for i in range(1, 4):
-        near_decay(i).wait_recv()
-    each_far_owner(lambda p, r: far_decay(p, r).start())
     near = jnp.zeros((8, 128), F32)
     for i in range(4):
         near = jnp.where(iota((8, 128), 0) == i, decay_all[quad * 4 + i], near)

time: 55.8 us -> 55.4 us (level)
  the two profiles are of different devices: /device:TPU:1 before, /device:TPU:25 now
where the time goes in v4:
time: 55.4 us; the launch traced here: 55.2 us
  Pallas kernels  55.2 us (100%)
    pallas_call x1, Pallas kernels, body(): pl.pallas_call(functools.partial(kernel, tp_size), out_shape=[pltpu.VMEM(...  54 us
    pallas_call x1, Pallas kernels, body(): pl.pallas_call(write, out_shape=jax.ShapeDtypeStruct((tokens, columns), B...  1.23 us

profile of v4, /device:TPU:25, one launch (start us, length us, event | category | flops | bytes accessed | tf_op | source)
XLA Modules:
  0.0 55.2 jit_solution(2642277957102130792)
XLA Ops:
  0.0 0.0 copy-start
  0.0 54.0 %shard_map.100 = (f32[4,768,256]{2,1,0:T(8,128)S(1)}, f32[768,128]{1,0:T(8,128)S(1)}) custom-call(s32[4]{0:T(128)} %len_hbm.1, bf16[768,1024]{1,0:T(8,128)(2,1)} %x_hbm.1, bf16[768,256]{1,0:T(8,128)(2,1)} %bc_hbm.1, bf16[768,1024]{1,0:T(8,128)(2,1)} %z_hbm.1, f32[16,768]{1,0:T(8,128)} %bitcast.8, f32[16,768]{1,0:T(8,128)} %bitcast.9, f32[1,16]{1,0:T(1,128)} %bitcast.11, ...), custom_call_target="tpu_custom_call" | custom-call | tf_op jit(solution)/shard_map/pallas_call | solution.py:780
  54.0 0.0 copy-done
  54.0 1.2 %shard_map.101 = bf16[768,1024]{1,0:T(8,128)(2,1)} custom-call(f32[4,768,256]{2,1,0:T(8,128)S(1)} %get-tuple-element.7.y_ref, f32[768,128]{1,0:T(8,128)S(1)} %get-tuple-element.8.scale_ref, f32[4,1,256]{2,1,0:T(1,128)S(1)} %bitcast.7), custom_call_target="tpu_custom_call" | custom-call | tf_op jit(solution)/shard_map/pallas_call | solution.py:868
Async XLA Ops:
  0.0 54.0 %copy-start = (f32[1024]{0:T(1024)S(1)}, f32[1024]{0:T(1024)}, u32[]{:S(2)}) copy-start(f32[1024]{0:T(1024)} %param.18) | copy-start | bytes 12292
